TPU v7x, 128 devices: a whole 4x4x4 slice. The times are simulated.
128 devices in a mesh: pos: 32 (over x, z, core), tile: 4 (over y).
Axes of the slice: x: 4, y: 4, z: 4, core: 2. Of those that a mesh axis runs over, the one named last changes fastest.
Arguments:
- object_slices: float32 [2, 2, 4096, 4096], P(None, None, 'pos', 'tile'), may hold values from -6 to 6
- probe: float32 [2, 256, 256], replicated, may hold values from -6 to 6
- patterns: float32 [128, 256, 256], P('pos'), may hold values from 0.25 to 4
- offsets: int32 [128, 2], P('pos'), may hold values from -128 to 896, as said below
- owner: int32 [128], P('pos'), may hold values from 0 to 3, as said below
Outputs:
- object_out: float32 [2, 2, 4096, 4096], P(None, None, 'pos', 'tile')
- probe_out: float32 [2, 256, 256], replicated
Inputs may be any that keep to these rules, and one draw needn't show every extreme that they name: Among the 4 positions of a band at most 2 have the same owner, and in every band one owner has exactly 2. `offsets`: rows are relative to the band's first row, columns to the owner tile's first column; every patch lies inside the object.
All inputs are finite; a program needn't handle non-finite values.
Results may differ from a plain program's by a relative error of at most 0.03.
Values may be sent and summed in bfloat16 or wider, within the bound.
A program may use at most 128 MiB of HBM per device.

v0:
```python
import math

import jax
import jax.numpy as jnp
from jax import lax
from jax.sharding import PartitionSpec as P

ITERS = 2
MOST = 2


fresnel = 0.05
eta_object = 0.5
eta_probe = 0.5


def from_behind(block, axis, distance):
    devices = range(lax.axis_size(axis))
    route = [(i - distance, i) for i in devices if i - distance in devices]
    return lax.ppermute(block, axis, route)


def with_halo(x, sides, width):
    for axis, dim in sides:
        size, length = (lax.axis_size(axis), x.shape[dim])
        up = [(i, (i + 1) % size) for i in range(size - 1)]
        down = [(j, i) for i, j in up]
        last = lax.slice_in_dim(x, length - width, length, axis=dim)
        leading = lax.slice_in_dim(x, 0, width, axis=dim)
        before = lax.ppermute(last, axis, up)
        after = lax.ppermute(leading, axis, down)
        x = jnp.concatenate([before, x, after], axis=dim)
    return x


def dft_tables(width):
    indices = jnp.arange(width, dtype=jnp.int32)
    product = indices[:, None] * indices[None, :] % width
    angles = product.astype(jnp.float32) * (2.0 * math.pi / width)
    factor = 1.0 / math.sqrt(width)
    cosine = (jnp.cos(angles) * factor).astype(jnp.bfloat16)
    sines = (jnp.sin(angles) * factor).astype(jnp.bfloat16)
    frequency = ((indices + width // 2) % width - width // 2).astype(jnp.float32)
    phases = -math.pi * fresnel / width * (frequency[:, None] ** 2 + frequency[None, :] ** 2)
    kernel = jnp.stack([jnp.cos(phases), jnp.sin(phases)])
    return (cosine, sines, kernel)


def section(field, cosine, sines, sign, on_left):
    if on_left:
        cos_part = jnp.einsum("jk,sckl->scjl", cosine, field, preferred_element_type=jnp.float32)
        sin_part = jnp.einsum("jk,sckl->scjl", sines, field, preferred_element_type=jnp.float32)
    else:
        cos_part = jnp.einsum("scjk,kl->scjl", field, cosine, preferred_element_type=jnp.float32)
        sin_part = jnp.einsum("scjk,kl->scjl", field, sines, preferred_element_type=jnp.float32)
    real_part = cos_part[:, 0] + sign * sin_part[:, 1]
    imag_part = cos_part[:, 1] - sign * sin_part[:, 0]
    return jnp.stack([real_part, imag_part], axis=1)


def transform(field, tables, sign):
    cosine, sines, kernel = tables
    middle = section(field.astype(jnp.bfloat16), cosine, sines, sign, False).astype(jnp.bfloat16)
    return section(middle, cosine, sines, sign, True)


def complex_product(first, second):
    real_part = (
        first[..., 0, :, :] * second[..., 0, :, :] - first[..., 1, :, :] * second[..., 1, :, :]
    )
    imag_part = (
        first[..., 0, :, :] * second[..., 1, :, :] + first[..., 1, :, :] * second[..., 0, :, :]
    )
    return jnp.stack([real_part, imag_part], axis=-3)


def conjugate_product(first, second):
    real_part = (
        first[..., 0, :, :] * second[..., 0, :, :] + first[..., 1, :, :] * second[..., 1, :, :]
    )
    imag_part = (
        first[..., 0, :, :] * second[..., 1, :, :] - first[..., 1, :, :] * second[..., 0, :, :]
    )
    return jnp.stack([real_part, imag_part], axis=-3)


def position_gradients(probe, patches, patterns, tables):
    slices = patches.astype(jnp.float32)
    count = slices.shape[1]
    kernel = tables[2]
    incoming = jnp.broadcast_to(probe, (slices.shape[0],) + probe.shape)
    waves = []
    leaving = incoming
    for level in range(count):
        waves.append(incoming)
        leaving = complex_product(incoming, slices[:, level])
        if level + 1 < count:
            incoming = transform(
                complex_product(kernel, transform(leaving, tables, 1.0)), tables, -1.0
            )
    farfield = transform(leaving, tables, 1.0)
    power = farfield[:, 0] ** 2 + farfield[:, 1] ** 2
    misfit = (power - patterns)[:, None] * farfield
    backward = transform(misfit, tables, -1.0)
    slice_grads = [None] * count
    upstream = backward
    for level in reversed(range(count)):
        slice_grads[level] = conjugate_product(waves[level], backward)
        upstream = conjugate_product(slices[:, level], backward)
        if level > 0:
            backward = transform(
                conjugate_product(kernel, transform(upstream, tables, 1.0)), tables, -1.0
            )
    return (jnp.stack(slice_grads, axis=1), upstream)


def rows_from(strip, offset):
    return from_behind(strip, "pos", offset)


def columns_from(strip, offset):
    return from_behind(strip, "tile", offset)


def fold_rows(grown, margin):
    inner = grown[:, :, margin:-margin]
    from_next = rows_from(grown[:, :, :margin], -1)
    from_prior = rows_from(grown[:, :, -margin:], 1)
    inner = inner.at[:, :, -margin:].add(from_next)
    return inner.at[:, :, :margin].add(from_prior)


def fold_columns(grown, margin):
    inner = grown[:, :, :, margin:-margin]
    from_next = columns_from(grown[:, :, :, :margin], -1)
    from_prior = columns_from(grown[:, :, :, -margin:], 1)
    inner = inner.at[:, :, :, -margin:].add(from_next)
    return inner.at[:, :, :, :margin].add(from_prior)


def per_device(object_slices, probe, patterns, offsets, owner):
    nslice, _, block_rows, block_cols = object_slices.shape
    width = probe.shape[-1]
    margin = width // 2
    band_count = patterns.shape[0]
    tables = dft_tables(width)
    zero = jnp.zeros((), jnp.int32)
    tile_here = lax.axis_index("tile")
    live = (owner == tile_here).astype(jnp.int32)
    ranks = jnp.cumsum(live) - live
    slot_ids = jnp.arange(MOST, dtype=jnp.int32)
    picked = ((live[None, :] == 1) & (ranks[None, :] == slot_ids[:, None])).astype(jnp.int32)
    chosen = jnp.sum(picked * jnp.arange(band_count, dtype=jnp.int32)[None, :], axis=1)
    valid = jnp.sum(picked, axis=1).astype(jnp.float32)
    slot_patterns = patterns[chosen]
    slot_rows = offsets[chosen, 0] + margin
    slot_cols = offsets[chosen, 1] + margin
    total_cells = float(
        nslice * 2 * block_rows * block_cols * lax.axis_size("pos") * lax.axis_size("tile")
    )
    field = object_slices
    current = probe
    for sweep in range(ITERS):
        lowered = field.astype(jnp.bfloat16)
        grown_object = with_halo(lowered, (("pos", 2), ("tile", 3)), margin)
        patches = jax.vmap(
            lambda r, c: lax.dynamic_slice(
                grown_object, (zero, zero, r, c), (nslice, 2, width, width)
            )
        )(slot_rows, slot_cols)
        slice_grads, probe_grads = position_gradients(current, patches, slot_patterns, tables)
        slice_grads = slice_grads * valid[:, None, None, None, None]
        local_probe = jnp.sum(probe_grads * valid[:, None, None, None], axis=0)

        def add_one(k, total):
            start = (zero, zero, slot_rows[k], slot_cols[k])
            before = lax.dynamic_slice(total, start, (nslice, 2, width, width))
            return lax.dynamic_update_slice(total, before + slice_grads[k], start)

        grown_grad = jnp.zeros(
            (nslice, 2, block_rows + 2 * margin, block_cols + 2 * margin), jnp.float32
        )
        grown_grad = lax.fori_loop(0, MOST, add_one, grown_grad)
        block_grad = fold_columns(fold_rows(grown_grad, margin), margin)
        probe_total, square_total = lax.psum(
            (local_probe, jnp.sum(block_grad * block_grad)), ("pos", "tile")
        )
        field = field - eta_object * lax.rsqrt(square_total / total_cells + 1e-06) * block_grad
        probe_square = jnp.sum(probe_total * probe_total) / float(2 * width * width)
        current = current - eta_probe * lax.rsqrt(probe_square + 1e-06) * probe_total
    return (field, current)


def solution(mesh):
    return jax.shard_map(
        per_device,
        mesh=mesh,
        in_specs=(
            P(None, None, "pos", "tile"),
            P(),
            P("pos", None, None),
            P("pos", None),
            P("pos"),
        ),
        out_specs=(P(None, None, "pos", "tile"), P()),
        check_vma=False,
    )
```

profile of v0, /device:TPU:1, one launch (start us, length us, event | category | flops | bytes accessed | tf_op | source)
XLA Modules:
  0.0 770.4 jit_solution(17162645407812919691)
XLA Ops:
  9.1 4.9 collective-permute-start
  14.0 1.9 collective-permute-start.1
  20.5 5.3 collective-permute-done
  25.7 4.7 collective-permute-done.1
  31.6 3.2 collective-permute-start.2
  36.3 3.2 collective-permute-done.2
  39.5 3.8 collective-permute-done.3
  43.4 3.3 pad_maximum_fusion
  46.8 7.1 while.42
  47.4 2.8 bitcast_dynamic-update-slice_fusion.4
  50.9 2.8 bitcast_dynamic-update-slice_fusion.4
  90.3 3.8 broadcast.522.clone
  94.1 37.0 %while.40 = (s32[]{:T(128)}, f32[2,2,384,1280]{3,2,1,0:T(8,128)}, s32[2]{0:T(128)S(1)}, s32[2]{0:T(128)S(1)}, f32[2,2,2,256,256]{4,3,2,0,1:T(8,128)S(1)}, /*index=5*/s32[]{:T(128)}, s32[]{:T(128)}, s32[]{:T(128)}, s32[]{:T(128)}) while((s32[]{:T(128)}, f32[2,2,384,1280]{3,2,1,0:T(8,128)}, s32[2]{0:T(128)S(1)}, s32[2]{0:T(128)S(1)}, ...), condition=%wide.region_4.5_spmd, body=%wide.region_3.4_spmd.sunk | while | flops 262152 | bytes 5243081 | solution.py:183
  100.9 11.4 %dynamic_update_slice.16 = f32[2,2,384,1280]{3,2,1,0:T(8,128)} dynamic-update-slice(f32[2,2,384,1280]{3,2,1,0:T(8,128)} %get-tuple-element.656, f32[2,2,256,256]{3,2,1,0:T(8,128)S(1)} %bitcast_add_fusion.4, s32[]{:T(128)} %constant.346.clone.1..sunk, s32[]{:T(128)} %constant.346.clone.1..sunk, s32[]{:T(128)S(6)} %select_n.307, s32[]{:T(128)S(6)} %select_n.308) | dynamic-update-slice | bytes 2097156 | tf_op jit(solution)/shard_map/while/body/eval_jaxpr/dynamic_update_slice | solution.py:178
  119.2 12.0 %dynamic_update_slice.16 = f32[2,2,384,1280]{3,2,1,0:T(8,128)} dynamic-update-slice(f32[2,2,384,1280]{3,2,1,0:T(8,128)} %get-tuple-element.656, f32[2,2,256,256]{3,2,1,0:T(8,128)S(1)} %bitcast_add_fusion.4, s32[]{:T(128)} %constant.346.clone.1..sunk, s32[]{:T(128)} %constant.346.clone.1..sunk, s32[]{:T(128)S(6)} %select_n.307, s32[]{:T(128)S(6)} %select_n.308) | dynamic-update-slice | bytes 2097156 | tf_op jit(solution)/shard_map/while/body/eval_jaxpr/dynamic_update_slice | solution.py:178
  131.2 2.9 fusion.451
  134.1 1.9 collective-permute-start.4
  136.0 6.6 collective-permute-start.5
  142.7 27.4 %collective-permute-done.4 = f32[2,2,128,1280]{3,2,1,0:T(8,128)S(1)} collective-permute-done((f32[2,2,128,1280]{3,2,1,0:T(8,128)S(1)}, f32[2,2,128,1280]{3,2,1,0:T(8,128)S(1)}, u32[]{:S(2)}, u32[]{:S(2)}) %collective-permute-start.4) | collective-permute-done | bytes 2621472 | tf_op jit(solution)/shard_map/ppermute | solution.py:20
  171.2 2.2 add_add_fusion.1
  174.8 4.0 collective-permute-start.7
  183.4 73.7 %psum.28 = f32[]{:T(128)} all-reduce(f32[]{:T(128)} %multiply_reduce_fusion.1), channel_id=1, replica_groups=mesh['pos'=32,'tile'=4] {'pos','tile'}, use_global_device_ids=true, to_apply=%region_6.7 | all-reduce | flops 1 | bytes 8 | tf_op jit(solution)/shard_map/psum | solution.py:185
  257.9 2.2 fusion.4
  260.1 1.9 collective-permute-start.8
  262.0 3.4 collective-permute-start.9
  266.4 146.7 %all-reduce.5.cloned.1.call-done = f32[2,256,256]{2,1,0:T(8,128)} async-done(((f32[2,256,256]{2,1,0:T(8,128)}), f32[2,256,256]{2,1,0:T(8,128)}) %all-reduce.5.cloned.1.call-update) | async-done | bytes 524304 | tf_op jit(solution)/shard_map/psum | solution.py:185
  416.9 2.3 collective-permute-start.10
  422.3 4.5 collective-permute-done.10
  426.8 3.8 collective-permute-done.11
  430.7 3.3 pad_maximum_fusion.1
  434.0 7.0 while.43
  434.7 2.7 bitcast_dynamic-update-slice_fusion.5
  438.0 2.7 bitcast_dynamic-update-slice_fusion.5
  479.4 3.8 broadcast.522
  483.2 37.8 %while.41 = (s32[]{:T(128)}, f32[2,2,384,1280]{3,2,1,0:T(8,128)}, s32[2]{0:T(128)S(1)}, s32[2]{0:T(128)S(1)}, f32[2,2,2,256,256]{4,3,2,0,1:T(8,128)}, /*index=5*/s32[]{:T(128)}, s32[]{:T(128)}, s32[]{:T(128)}, s32[]{:T(128)}) while((s32[]{:T(128)}, f32[2,2,384,1280]{3,2,1,0:T(8,128)}, s32[2]{0:T(128)S(1)}, s32[2]{0:T(128)S(1)}, ...), condition=%wide.region_11.12_spmd, body=%wide.region_10.11_spmd.sunk | while | flops 262152 | bytes 5243081 | solution.py:183
  488.2 2.1 bitcast_add_fusion.5
  490.4 11.4 %dynamic_update_slice.17 = f32[2,2,384,1280]{3,2,1,0:T(8,128)} dynamic-update-slice(f32[2,2,384,1280]{3,2,1,0:T(8,128)} %get-tuple-element.698, f32[2,2,256,256]{3,2,1,0:T(8,128)S(1)} %bitcast_add_fusion.5, s32[]{:T(128)} %constant.346.clone.1..sunk.1, s32[]{:T(128)} %constant.346.clone.1..sunk.1, s32[]{:T(128)S(6)} %select_n.309, s32[]{:T(128)S(6)} %select_n.310) | dynamic-update-slice | bytes 2097156 | tf_op jit(solution)/shard_map/while/body/eval_jaxpr/dynamic_update_slice | solution.py:178
  506.8 2.1 bitcast_add_fusion.5
  509.0 12.0 %dynamic_update_slice.17 = f32[2,2,384,1280]{3,2,1,0:T(8,128)} dynamic-update-slice(f32[2,2,384,1280]{3,2,1,0:T(8,128)} %get-tuple-element.698, f32[2,2,256,256]{3,2,1,0:T(8,128)S(1)} %bitcast_add_fusion.5, s32[]{:T(128)} %constant.346.clone.1..sunk.1, s32[]{:T(128)} %constant.346.clone.1..sunk.1, s32[]{:T(128)S(6)} %select_n.309, s32[]{:T(128)S(6)} %select_n.310) | dynamic-update-slice | bytes 2097156 | tf_op jit(solution)/shard_map/while/body/eval_jaxpr/dynamic_update_slice | solution.py:178
  521.0 5.3 fusion.450
  526.3 2.0 collective-permute-start.12
  528.3 4.7 collective-permute-start.13
  534.0 27.7 %collective-permute-done.12 = f32[2,2,128,1280]{3,2,1,0:T(8,128)} collective-permute-done((f32[2,2,128,1280]{3,2,1,0:T(8,128)}, f32[2,2,128,1280]{3,2,1,0:T(8,128)}, u32[]{:S(2)}, u32[]{:S(2)}) %collective-permute-start.12) | collective-permute-done | bytes 2621472 | tf_op jit(solution)/shard_map/ppermute | solution.py:20
  562.7 3.8 add_add_fusion
  570.0 4.3 collective-permute-start.15
  574.3 111.2 %all-reduce.7.cloned.1.call-done = f32[2,256,256]{2,1,0:T(8,128)} async-done(((f32[2,256,256]{2,1,0:T(8,128)}), f32[2,256,256]{2,1,0:T(8,128)}) %all-reduce.7.cloned.1.call-update) | async-done | bytes 524304 | tf_op jit(solution)/shard_map/psum | solution.py:185
  694.1 63.9 %psum.30 = f32[]{:T(128)} all-reduce(f32[]{:T(128)} %multiply_reduce_fusion), channel_id=1, replica_groups=mesh['pos'=32,'tile'=4] {'pos','tile'}, use_global_device_ids=true, to_apply=%region_13.14 | all-reduce | flops 1 | bytes 8 | tf_op jit(solution)/shard_map/psum | solution.py:185
  758.7 4.6 multiply_subtract_fusion
  (220 shorter events, 122.2 us)
Async XLA Ops:
  7.2 10.7 %copy-start = (f32[4,256,256]{2,1,0:T(8,128)S(1)}, f32[4,256,256]{2,1,0:T(8,128)}, u32[]{:S(2)}) copy-start(f32[4,256,256]{2,1,0:T(8,128)} %param.35) | copy-start | bytes 3145732
  7.2 8.8 %copy-start.25 = (s32[4]{0:T(128)S(1)}, s32[4]{0:T(128)}, u32[]{:S(2)}) copy-start(s32[4]{0:T(128)} %param.37) | copy-start | bytes 52
  7.2 9.1 %copy-start.2 = (s32[4,2]{0,1:T(2,128)S(1)}, s32[4,2]{0,1:T(2,128)}, u32[]{:S(2)}) copy-start(s32[4,2]{0,1:T(2,128)} %param.36) | copy-start | bytes 100
  7.2 405.9 %all-reduce.5.cloned.1.call-start = ((), (), s32[]{:S(2)}) async-start(), calls=%async_computation | async-start | bytes 1048576 | tf_op jit(solution)/shard_map/psum | solution.py:185
  9.1 16.7 %collective-permute-start = (bf16[2,2,128,1024]{3,2,1,0:T(8,128)(2,1)S(1)}, bf16[2,2,128,1024]{3,2,1,0:T(8,128)(2,1)}, u32[]{:S(2)}, u32[]{:S(2)}) collective-permute-start(bf16[2,2,128,1024]{3,2,1,0:T(8,128)(2,1)S(1)} %convert_element_type.295), channel_id=1, source_target_pairs={{0,4},{4,8},{8,12},{12,16},{16,20},{20,24},{24,28},{28,32},{32,36}... | collective-permute-start | bytes 3145736 | tf_op jit(solution)/shard_map/ppermute | solution.py:30
  14.0 16.4 %collective-permute-start.1 = (bf16[2,2,128,1024]{3,2,1,0:T(8,128)(2,1)S(1)}, bf16[2,2,128,1024]{3,2,1,0:T(8,128)(2,1)}, u32[]{:S(2)}, u32[]{:S(2)}) collective-permute-start(bf16[2,2,128,1024]{3,2,1,0:T(8,128)(2,1)S(1)} %convert_element_type.295), channel_id=1, source_target_pairs={{4,0},{8,4},{12,8},{16,12},{20,16},{24,20},{28,24},{32,28},{36,32}... | collective-permute-start | bytes 3145736 | tf_op jit(solution)/shard_map/ppermute | solution.py:31
  18.4 17.8 %copy-start.19 = (f32[2,256,256]{2,1,0:T(8,128)S(1)}, f32[2,256,256]{2,1,0:T(8,128)}, u32[]{:S(2)}) copy-start(f32[2,256,256]{2,1,0:T(8,128)} %param.34) | copy-start | bytes 1572868
  20.5 62.0 %copy-start.5 = (f32[256,256]{0,1:T(8,128)}, f32[256,256]{0,1:T(8,128)S(1)}, u32[]{:S(2)}) copy-start(f32[256,256]{0,1:T(8,128)S(1)} %get-tuple-element.501) | copy-start | bytes 786436
  31.6 7.9 %collective-permute-start.2 = (bf16[2,2,384,128]{3,2,1,0:T(8,128)(2,1)S(1)}, bf16[2,2,384,128]{3,2,1,0:T(8,128)(2,1)S(1)}, u32[]{:S(2)}, u32[]{:S(2)}) collective-permute-start(bf16[2,2,384,128]{3,2,1,0:T(8,128)(2,1)S(1)} %get-tuple-element.438), channel_id=1, source_target_pairs={{0,1},{1,2},{2,3},{4,5},{5,6},{6,7},{8,9},{9,10},{10,11},{12,13},{... | collective-permute-start | bytes 1179656 | tf_op jit(solution)/shard_map/ppermute | solution.py:30
  34.9 8.5 %collective-permute-start.3 = (bf16[2,2,384,128]{3,2,1,0:T(8,128)(2,1)S(1)}, bf16[2,2,384,128]{3,2,1,0:T(8,128)(2,1)S(1)}, u32[]{:S(2)}, u32[]{:S(2)}) collective-permute-start(bf16[2,2,384,128]{3,2,1,0:T(8,128)(2,1)S(1)} %get-tuple-element.439), channel_id=1, source_target_pairs={{1,0},{2,1},{3,2},{5,4},{6,5},{7,6},{9,8},{10,9},{11,10},{13,12},{... | collective-permute-start | bytes 1179656 | tf_op jit(solution)/shard_map/ppermute | solution.py:31
  36.3 17.9 %copy-start.13 = (f32[256,256]{1,0:T(8,128)}, f32[256,256]{1,0:T(8,128)S(1)}, u32[]{:S(2)}) copy-start(f32[256,256]{1,0:T(8,128)S(1)} %get-tuple-element.498) | copy-start | bytes 786436
  36.3 17.9 %copy-start.15 = (f32[256,256]{1,0:T(8,128)}, f32[256,256]{1,0:T(8,128)S(1)}, u32[]{:S(2)}) copy-start(f32[256,256]{1,0:T(8,128)S(1)} %get-tuple-element.499) | copy-start | bytes 786436
  68.5 2.6 copy-start.9
  87.8 1.0 copy-start.14
  87.8 1.0 copy-start.16
  134.1 35.9 %collective-permute-start.4 = (f32[2,2,128,1280]{3,2,1,0:T(8,128)S(1)}, f32[2,2,128,1280]{3,2,1,0:T(8,128)S(1)}, u32[]{:S(2)}, u32[]{:S(2)}) collective-permute-start(f32[2,2,128,1280]{3,2,1,0:T(8,128)S(1)} %get-tuple-element.434), channel_id=1, source_target_pairs={{4,0},{8,4},{12,8},{16,12},{20,16},{24,20},{28,24},{32,28},{36,32}... | collective-permute-start | bytes 7864328 | tf_op jit(solution)/shard_map/ppermute | solution.py:20
  136.0 35.2 %collective-permute-start.5 = (f32[2,2,128,1280]{3,2,1,0:T(8,128)S(1)}, f32[2,2,128,1280]{3,2,1,0:T(8,128)S(1)}, u32[]{:S(2)}, u32[]{:S(2)}) collective-permute-start(f32[2,2,128,1280]{3,2,1,0:T(8,128)S(1)} %get-tuple-element.435), channel_id=1, source_target_pairs={{0,4},{4,8},{8,12},{12,16},{16,20},{20,24},{24,28},{28,32},{32,36}... | collective-permute-start | bytes 7864328 | tf_op jit(solution)/shard_map/ppermute | solution.py:20
  173.5 7.1 collective-permute-start.6
  174.8 7.3 collective-permute-start.7
  257.8 7.6 copy-start.17
  257.8 7.5 copy-start.23
  260.1 155.5 %collective-permute-start.8 = (bf16[2,2,128,1024]{3,2,1,0:T(8,128)(2,1)S(1)}, bf16[2,2,128,1024]{3,2,1,0:T(8,128)(2,1)}, u32[]{:S(2)}, u32[]{:S(2)}) collective-permute-start(bf16[2,2,128,1024]{3,2,1,0:T(8,128)(2,1)S(1)} %fusion.4), channel_id=1, source_target_pairs={{0,4},{4,8},{8,12},{12,16},{16,20},{20,24},{24,28},{28,32},{32,36}... | collective-permute-start | bytes 3145736 | tf_op jit(solution)/shard_map/ppermute | solution.py:30
  262.0 153.6 %collective-permute-start.9 = (bf16[2,2,128,1024]{3,2,1,0:T(8,128)(2,1)S(1)}, bf16[2,2,128,1024]{3,2,1,0:T(8,128)(2,1)}, u32[]{:S(2)}, u32[]{:S(2)}) collective-permute-start(bf16[2,2,128,1024]{3,2,1,0:T(8,128)(2,1)S(1)} %fusion.4), channel_id=1, source_target_pairs={{4,0},{8,4},{12,8},{16,12},{20,16},{24,20},{28,24},{32,28},{36,32}... | collective-permute-start | bytes 3145736 | tf_op jit(solution)/shard_map/ppermute | solution.py:31
  266.4 419.1 %all-reduce.7.cloned.1.call-start = ((), (), s32[]{:S(2)}) async-start(), calls=%async_computation.1 | async-start | bytes 1048576 | tf_op jit(solution)/shard_map/psum | solution.py:185
  415.6 5.0 copy-start.20
  415.6 5.0 copy-start.22
  416.9 9.9 %collective-permute-start.10 = (bf16[2,2,384,128]{3,2,1,0:T(8,128)(2,1)S(1)}, bf16[2,2,384,128]{3,2,1,0:T(8,128)(2,1)S(1)}, u32[]{:S(2)}, u32[]{:S(2)}) collective-permute-start(bf16[2,2,384,128]{3,2,1,0:T(8,128)(2,1)S(1)} %get-tuple-element.436), channel_id=1, source_target_pairs={{0,1},{1,2},{2,3},{4,5},{5,6},{6,7},{8,9},{9,10},{10,11},{12,13},{... | collective-permute-start | bytes 1179656 | tf_op jit(solution)/shard_map/ppermute | solution.py:30
  419.2 11.4 %collective-permute-start.11 = (bf16[2,2,384,128]{3,2,1,0:T(8,128)(2,1)S(1)}, bf16[2,2,384,128]{3,2,1,0:T(8,128)(2,1)S(1)}, u32[]{:S(2)}, u32[]{:S(2)}) collective-permute-start(bf16[2,2,384,128]{3,2,1,0:T(8,128)(2,1)S(1)} %get-tuple-element.437), channel_id=1, source_target_pairs={{1,0},{2,1},{3,2},{5,4},{6,5},{7,6},{9,8},{10,9},{11,10},{13,12},{... | collective-permute-start | bytes 1179656 | tf_op jit(solution)/shard_map/ppermute | solution.py:31
  420.6 0.8 copy-start.7
  441.3 1.0 copy-start.11
  441.3 1.0 copy-start.12
  445.2 2.6 copy-start.6
  456.4 2.6 copy-start.10
  521.0 12.1 %copy-start.18 = (f32[2,1,256,256]{3,2,1,0:T(8,128)S(1)}, f32[2,1,256,256]{3,2,1,0:T(8,128)}, u32[]{:S(2)}) copy-start(f32[2,1,256,256]{3,2,1,0:T(8,128)} %get-tuple-element.404) | copy-start | bytes 1572868
  521.0 12.1 %copy-start.24 = (f32[2,1,256,256]{3,2,1,0:T(8,128)S(1)}, f32[2,1,256,256]{3,2,1,0:T(8,128)}, u32[]{:S(2)}) copy-start(f32[2,1,256,256]{3,2,1,0:T(8,128)} %get-tuple-element.492) | copy-start | bytes 1572868
  526.3 35.4 %collective-permute-start.12 = (f32[2,2,128,1280]{3,2,1,0:T(8,128)}, f32[2,2,128,1280]{3,2,1,0:T(8,128)}, u32[]{:S(2)}, u32[]{:S(2)}) collective-permute-start(f32[2,2,128,1280]{3,2,1,0:T(8,128)} %get-tuple-element.432), channel_id=1, source_target_pairs={{4,0},{8,4},{12,8},{16,12},{20,16},{24,20},{28,24},{32,28},{36,32}... | collective-permute-start | bytes 7864328 | tf_op jit(solution)/shard_map/ppermute | solution.py:20
  528.3 34.3 %collective-permute-start.13 = (f32[2,2,128,1280]{3,2,1,0:T(8,128)}, f32[2,2,128,1280]{3,2,1,0:T(8,128)}, u32[]{:S(2)}, u32[]{:S(2)}) collective-permute-start(f32[2,2,128,1280]{3,2,1,0:T(8,128)} %get-tuple-element.433), channel_id=1, source_target_pairs={{0,4},{4,8},{8,12},{12,16},{16,20},{20,24},{24,28},{28,32},{32,36}... | collective-permute-start | bytes 7864328 | tf_op jit(solution)/shard_map/ppermute | solution.py:20
  566.4 1.5 copy-start.3
  568.7 119.3 %collective-permute-start.14 = (f32[2,2,128,128]{3,2,1,0:T(8,128)}, f32[2,2,128,128]{3,2,1,0:T(8,128)}, u32[]{:S(2)}, u32[]{:S(2)}) collective-permute-start(f32[2,2,128,128]{3,2,1,0:T(8,128)} %get-tuple-element.441), channel_id=1, source_target_pairs={{1,0},{2,1},{3,2},{5,4},{6,5},{7,6},{9,8},{10,9},{11,10},{13,12},{... | collective-permute-start | bytes 786440 | tf_op jit(solution)/shard_map/ppermute | solution.py:20
  570.0 120.6 %collective-permute-start.15 = (f32[2,2,128,128]{3,2,1,0:T(8,128)}, f32[2,2,128,128]{3,2,1,0:T(8,128)S(1)}, u32[]{:S(2)}, u32[]{:S(2)}) collective-permute-start(f32[2,2,128,128]{3,2,1,0:T(8,128)} %get-tuple-element.440), channel_id=1, source_target_pairs={{0,1},{1,2},{2,3},{4,5},{5,6},{6,7},{8,9},{9,10},{10,11},{12,13},{... | collective-permute-start | bytes 786440 | tf_op jit(solution)/shard_map/ppermute | solution.py:20
  688.0 1.6 slice-start
  688.0 5.3 copy-start.8
  688.0 5.3 copy-start.21
  690.7 1.3 copy-start.4
  758.7 4.6 copy-start.1
Sparse Core Ops, SparseCore 0:
  266.5 146.5 all-reduce.4
  534.1 151.3 all-reduce.6
where the time goes:
time: 776 us; the launch traced here: 770 us
  waiting for transfers between devices  344 us (44%)
  blocking collectives  138 us (18%)
  local copies, waits for them, and re-layouts  92.8 us (12%)
  matrix products  61.1 us (8%)
  other arithmetic  55 us (7%)
  starting transfers between devices  46.5 us (6%)
  between operations  18.2 us (2%)
  loops' own time  15.7 us (2%)
    psum x2, waiting for transfers between devices, per_device(): lax.psum((local_probe, jnp.sum(block_grad * block_grad)), ('pos', 'tile'))  258 us
    psum x2, blocking collectives, per_device(): lax.psum((local_probe, jnp.sum(block_grad * block_grad)), ('pos', 'tile'))  138 us
    ppermute x8, waiting for transfers between devices, from_behind(): return lax.ppermute(block, axis, route)  60.2 us
    dynamic_update_slice x4, local copies, waits for them, and re-layouts, add_one(): return lax.dynamic_update_slice(total, before + slice_grads[k], start)  46.8 us
    ppermute x8, starting transfers between devices, from_behind(): return lax.ppermute(block, axis, route)  26.1 us
    dot_general x12, matrix products, section(): jnp.einsum('scjk,kl->scjl', field, cosine, preferred_element_type=jnp.flo...  15.7 us
    dot_general x12, matrix products, section(): jnp.einsum('scjk,kl->scjl', field, sines, preferred_element_type=jnp.floa...  15.5 us
  transfers between devices with their start and end apart: 18, of which 14 were waited for; matrix products, arithmetic and copies ran while one was open for 2% of the time, Pallas kernels for 0%

commit v1 on v0

v1 whole, which is shorter than its diff:
```python
import functools
import math

import jax
import jax.numpy as jnp
import numpy as np
from jax import lax
from jax.experimental import pallas as pl
from jax.experimental.pallas import tpu as pltpu
from jax.sharding import PartitionSpec as P

ITERS = 2
MOST = 2
FRESNEL = 0.05
ETA_OBJECT = 0.5
ETA_PROBE = 0.5
W = 256
M = 128
MESH = pl.DeviceIdType.MESH
F32 = jnp.float32
BF16 = jnp.bfloat16


def tables():
    indices = np.arange(W)
    angles = (indices[:, None] * indices[None, :] % W) * (2.0 * math.pi / W)
    cosine = np.cos(angles) / math.sqrt(W)
    sine = np.sin(angles) / math.sqrt(W)
    ahead = np.block([[cosine, -sine], [sine, cosine]])
    behind = np.block([[cosine, sine], [-sine, cosine]])
    dft = np.stack([ahead, behind]).astype(np.float32).astype(jnp.bfloat16)
    frequency = ((indices + W // 2) % W - W // 2).astype(np.float32)
    phases = -math.pi * FRESNEL / W * (frequency[:, None] ** 2 + frequency[None, :] ** 2)
    spread = np.stack([np.cos(phases), np.sin(phases)]).astype(np.float32)
    return dft, spread


def slot_info(owner_of, offset_of, bands, tile):
    zero = jnp.int32(0)
    found = zero
    slots = [[zero, zero, zero, zero] for _ in range(MOST)]
    for n in range(bands):
        live = owner_of(n) == tile
        row, col = offset_of(n, 0) + M, offset_of(n, 1) + M
        for k in range(MOST):
            here = jnp.logical_and(live, found == k)
            slots[k] = [
                jnp.where(here, new, old)
                for new, old in zip((row, col, jnp.int32(n), jnp.int32(1)), slots[k])
            ]
        found = found + live.astype(jnp.int32)
    return slots


def one_hot(rows, cols, shift):
    row = lax.broadcasted_iota(jnp.int32, (rows, cols), 0)
    col = lax.broadcasted_iota(jnp.int32, (rows, cols), 1)
    return (row == col + shift).astype(F32).astype(BF16)


def dot(a, b):
    return jnp.dot(a, b, preferred_element_type=F32)


def body(sizes, *refs):
    (npos, ntile, nw, bands, block_cols, cells) = sizes
    (off, own, obj, probe_in, pats_in, tab_in, spread_in, obj_out, probe_out) = refs[:9]
    (
        off_nb, own_nb, fld, acc, low, parts, halo_send, fold_send, contrib, edge_send, edge_recv,
        probe, pats, tab, spread, place, rows_in, rows_out, patch, x, mid, psi1, pg,
        rs1_send, rs1, rs2_send, rs2, ag_send, ag, sq_a, sq_b, sq_sa, sq_sb,
        local_sem, info_s, info_r, col_s, col_r, halo_s, halo_r, fold_s, fold_r, edge_s, edge_r,
        p_s, p_r, q_s, q_r,
    ) = refs[9:]
    grown = block_cols + 2 * M
    nx = npos // nw
    ng = nx * ntile
    p = lax.axis_index("pos")
    t = lax.axis_index("tile")
    xi, wi = p // nw, p % nw
    me_g = xi * ntile + t

    up = {"pos": lax.rem(p + npos - 1, npos)}
    down = {"pos": lax.rem(p + 1, npos)}
    left = {"tile": lax.rem(t + ntile - 1, ntile)}
    right = {"tile": lax.rem(t + 1, ntile)}

    def g_peer(j):
        return {
            "pos": lax.rem(xi + j // ntile, nx) * nw + wi,
            "tile": lax.rem(t + j % ntile, ntile),
        }

    def g_index(j):
        return lax.rem(xi + j // ntile, nx) * ntile + lax.rem(t + j % ntile, ntile)

    def w_peer(j):
        return {"pos": xi * nw + lax.rem(wi + j, nw)}

    def remote(src, dst, send, recv, where):
        return pltpu.make_async_remote_copy(
            src_ref=src, dst_ref=dst, send_sem=send, recv_sem=recv, device_id=where, device_id_type=MESH
        )

    def wait_bytes(ref, sem):
        pltpu.make_async_copy(ref, ref, sem).wait()

    loads = [
        pltpu.make_async_copy(obj, fld.at[:, :, pl.ds(M, block_cols)], local_sem.at[0]),
        pltpu.make_async_copy(probe_in, probe, local_sem.at[1]),
        pltpu.make_async_copy(tab_in, tab, local_sem.at[2]),
        pltpu.make_async_copy(spread_in, spread, local_sem.at[3]),
        pltpu.make_async_copy(pats_in, pats, local_sem.at[4]),
    ]
    for load in loads:
        load.start()

    barrier = pltpu.get_barrier_semaphore()
    friends = [up, down, left, right]
    friends += [g_peer(j) for j in range(1, ng)]
    friends += [w_peer(j) for j in range(1, nw)]
    for friend in friends:
        pl.semaphore_signal(barrier, inc=1, device_id=friend, device_id_type=MESH)
    pl.semaphore_wait(barrier, len(friends))

    info = [
        remote(off, off_nb.at[0], info_s.at[0], info_r.at[0], down),
        remote(own, own_nb.at[0], info_s.at[1], info_r.at[1], down),
        remote(off, off_nb.at[1], info_s.at[2], info_r.at[2], up),
        remote(own, own_nb.at[1], info_s.at[3], info_r.at[3], up),
    ]
    cols = [
        remote(obj.at[:, :, pl.ds(block_cols - M, M)], fld.at[:, :, pl.ds(0, M)], col_s.at[0], col_r.at[0], right),
        remote(obj.at[:, :, pl.ds(0, M)], fld.at[:, :, pl.ds(M + block_cols, M)], col_s.at[1], col_r.at[1], left),
    ]
    for copy in info + cols:
        copy.start()

    mine = slot_info(lambda n: own[n], lambda n, i: off[n, i], bands, t)
    for k in range(MOST):
        rows_in[k] = (
            lax.broadcasted_iota(jnp.int32, (W, 3 * M), 1)
            == lax.broadcasted_iota(jnp.int32, (W, 3 * M), 0) + mine[k][0]
        ).astype(F32).astype(BF16)
        rows_out[k] = one_hot(3 * M, W, mine[k][0])
    for copy in info:
        copy.wait_recv()
    above = slot_info(lambda n: own_nb[0, n], lambda n, i: off_nb[0, n, i], bands, t)
    below = slot_info(lambda n: own_nb[1, n], lambda n, i: off_nb[1, n, i], bands, t)
    slots = above + mine + below
    for k in range(3 * MOST):
        place[pl.ds(k * W, W), :] = (
            lax.broadcasted_iota(jnp.int32, (W, grown), 1)
            == lax.broadcasted_iota(jnp.int32, (W, grown), 0) + slots[k][1]
        ).astype(F32).astype(BF16)
    for copy in cols:
        copy.wait_recv()
    for load in loads:
        load.wait()

    sends = info + cols

    def transform(k, way):
        half = dot(x[k], tab[way]).astype(BF16)
        mid[k, pl.ds(0, W)] = half[:, :W]
        mid[k, pl.ds(W, W)] = half[:, W:]
        both = dot(tab[1 - way], mid[k])
        return both[:W], both[W:]

    def put(k, re, im):
        x[k, :, pl.ds(0, W)] = re.astype(BF16)
        x[k, :, pl.ds(W, W)] = im.astype(BF16)

    for it in range(ITERS):
        low[...] = fld[...].astype(BF16)

        def chosen(k):
            return lax.dot_general(
                low[...].reshape(4 * M, grown),
                place[pl.ds(k * W, W), :],
                (((1,), (1,)), ((), ())),
                preferred_element_type=F32,
            ).astype(BF16).reshape(4, M, W)

        for k in range(MOST):
            halo_send[it, 0, k] = chosen(k)
            halo_send[it, 1, k] = chosen(2 * MOST + k)
        halo = [
            remote(halo_send.at[it, 0], parts.at[it, 2], halo_s.at[it, 0], halo_r.at[it, 0], up),
            remote(halo_send.at[it, 1], parts.at[it, 0], halo_s.at[it, 1], halo_r.at[it, 1], down),
        ]
        for copy in halo:
            copy.start()
        sends += halo
        for k in range(MOST):
            parts[it, 1, k] = chosen(MOST + k)
        for copy in halo:
            copy.wait_recv()
        for k in range(MOST):
            for c in range(4):
                stack = jnp.concatenate([parts[it, 0, k, c], parts[it, 1, k, c], parts[it, 2, k, c]], axis=0)
                patch[k, c] = dot(rows_in[k], stack)

        for k in range(MOST):
            re = probe[0] * patch[k, 0] - probe[1] * patch[k, 1]
            im = probe[0] * patch[k, 1] + probe[1] * patch[k, 0]
            put(k, re, im)
        for k in range(MOST):
            a, b = transform(k, 0)
            put(k, spread[0] * a - spread[1] * b, spread[0] * b + spread[1] * a)
        for k in range(MOST):
            a, b = transform(k, 1)
            psi1[k, 0] = a
            psi1[k, 1] = b
            put(k, a * patch[k, 2] - b * patch[k, 3], a * patch[k, 3] + b * patch[k, 2])
        for k in range(MOST):
            a, b = transform(k, 0)
            wanted = jnp.zeros((W, W), F32)
            for n in range(bands):
                wanted = jnp.where(mine[k][2] == n, pats[n], wanted)
            misfit = a * a + b * b - wanted
            put(k, misfit * a, misfit * b)

        def fold_out(k, c, value):
            value = jnp.where(mine[k][3] > 0, value, 0.0).astype(BF16)
            rows = dot(rows_out[k], value).astype(BF16)
            fold_send[it, 0, k, c] = rows[:M]
            contrib[it, 1, k, c] = rows[M : 2 * M]
            fold_send[it, 1, k, c] = rows[2 * M :]

        for k in range(MOST):
            a, b = transform(k, 1)
            put(k, patch[k, 2] * a + patch[k, 3] * b, patch[k, 2] * b - patch[k, 3] * a)
            fold_out(k, 2, psi1[k, 0] * a + psi1[k, 1] * b)
            fold_out(k, 3, psi1[k, 0] * b - psi1[k, 1] * a)
        for k in range(MOST):
            a, b = transform(k, 0)
            put(k, spread[0] * a + spread[1] * b, spread[0] * b - spread[1] * a)
        for k in range(MOST):
            a, b = transform(k, 1)
            fold_out(k, 0, probe[0] * a + probe[1] * b)
            fold_out(k, 1, probe[0] * b - probe[1] * a)
            re = jnp.where(mine[k][3] > 0, patch[k, 0] * a + patch[k, 1] * b, 0.0)
            im = jnp.where(mine[k][3] > 0, patch[k, 0] * b - patch[k, 1] * a, 0.0)
            if k == 0:
                pg[pl.ds(0, W)] = re
                pg[pl.ds(W, W)] = im
            else:
                pg[pl.ds(0, W)] = pg[pl.ds(0, W)] + re
                pg[pl.ds(W, W)] = pg[pl.ds(W, W)] + im

        fold = [
            remote(fold_send.at[it, 0], contrib.at[it, 2], fold_s.at[it, 0], fold_r.at[it, 0], up),
            remote(fold_send.at[it, 1], contrib.at[it, 0], fold_s.at[it, 1], fold_r.at[it, 1], down),
        ]
        for copy in fold:
            copy.start()
        sends += fold
        chunk = 2 * W // ng
        rs1_send[it] = pg[...].astype(BF16).reshape(ng, chunk, W)
        for j in range(1, ng):
            remote(
                rs1_send.at[it, g_index(j)], rs1.at[it, me_g], p_s.at[it, 0], p_r.at[it, 0], g_peer(j)
            ).start()
        rs1[it, me_g] = rs1_send[it, me_g]

        for copy in fold:
            copy.wait_recv()
        terms = jnp.concatenate(
            [contrib[it, s, k].reshape(4 * M, W) for s in range(3) for k in range(MOST)], axis=1
        )
        for start in (0, grown - W):
            acc[:, :, pl.ds(start, W)] = dot(terms, place[:, pl.ds(start, W)]).reshape(4, M, W)
        edge_send[it, 0] = acc[:, :, pl.ds(0, W)].astype(BF16)
        edge_send[it, 1] = acc[:, :, pl.ds(grown - W, W)].astype(BF16)
        edge = [
            remote(edge_send.at[it, 0], edge_recv.at[it, 1], edge_s.at[it, 0], edge_r.at[it, 0], left),
            remote(edge_send.at[it, 1], edge_recv.at[it, 0], edge_s.at[it, 1], edge_r.at[it, 1], right),
        ]
        for copy in edge:
            copy.start()
        sends += edge
        for start in range(W, grown - W, W):
            acc[:, :, pl.ds(start, W)] = dot(terms, place[:, pl.ds(start, W)]).reshape(4, M, W)

        wait_bytes(rs1.at[it, pl.ds(0, ng - 1)], p_r.at[it, 0])
        rs2_send[it] = jnp.sum(rs1[it].astype(F32), axis=0).astype(BF16)
        for j in range(1, nw):
            remote(rs2_send.at[it], rs2.at[it, wi], p_s.at[it, 1], p_r.at[it, 1], w_peer(j)).start()
        rs2[it, wi] = rs2_send[it]

        for copy in edge:
            copy.wait_recv()
        acc[:, :, pl.ds(0, W)] = acc[:, :, pl.ds(0, W)] + edge_recv[it, 0].astype(F32)
        acc[:, :, pl.ds(grown - W, W)] = acc[:, :, pl.ds(grown - W, W)] + edge_recv[it, 1].astype(F32)
        inner = acc[:, :, pl.ds(M, block_cols)].reshape(4 * M, block_cols)
        squares = jnp.sum((inner * inner).reshape(4 * M // 8, 8, block_cols), axis=0)
        total = squares[:, :M]
        for i in range(1, block_cols // M):
            total = total + squares[:, i * M : (i + 1) * M]
        sq_sa[it] = total
        for j in range(1, ng):
            remote(sq_sa.at[it], sq_a.at[it, me_g], q_s.at[it, 0], q_r.at[it, 0], g_peer(j)).start()
        sq_a[it, me_g] = sq_sa[it]

        wait_bytes(rs2.at[it, pl.ds(0, nw - 1)], p_r.at[it, 1])
        ag_send[it] = jnp.sum(rs2[it].astype(F32), axis=0).astype(BF16)
        for j in range(1, ng):
            remote(ag_send.at[it], ag.at[it, me_g], p_s.at[it, 2], p_r.at[it, 2], g_peer(j)).start()
        ag[it, me_g] = ag_send[it]

        wait_bytes(sq_a.at[it, pl.ds(0, ng - 1)], q_r.at[it, 0])
        sq_sb[it] = jnp.sum(sq_a[it], axis=0)
        for j in range(1, nw):
            remote(sq_sb.at[it], sq_b.at[it, wi], q_s.at[it, 1], q_r.at[it, 1], w_peer(j)).start()
        sq_b[it, wi] = sq_sb[it]

        wait_bytes(ag.at[it, pl.ds(0, ng - 1)], p_r.at[it, 2])
        grad = ag[it].astype(F32).reshape(2, W, W)
        mean = jnp.sum(grad * grad) / float(2 * W * W)
        probe[...] = probe[...] - ETA_PROBE * lax.rsqrt(mean + 1e-06) * grad

        wait_bytes(sq_b.at[it, pl.ds(0, nw - 1)], q_r.at[it, 1])
        mean = jnp.sum(jnp.sum(sq_b[it], axis=0)) / cells
        fld[...] = fld[...] - ETA_OBJECT * lax.rsqrt(mean + 1e-06) * acc[...]

    stores = [
        pltpu.make_async_copy(fld.at[:, :, pl.ds(M, block_cols)], obj_out, local_sem.at[0]),
        pltpu.make_async_copy(probe, probe_out, local_sem.at[1]),
    ]
    for store in stores:
        store.start()
    for copy in sends:
        copy.wait_send()
    for it in range(ITERS):
        wait_bytes(rs1_send.at[it, pl.ds(0, ng - 1)], p_s.at[it, 0])
        wait_bytes(rs2.at[it, pl.ds(0, nw - 1)], p_s.at[it, 1])
        wait_bytes(ag.at[it, pl.ds(0, ng - 1)], p_s.at[it, 2])
        wait_bytes(sq_a.at[it, pl.ds(0, ng - 1)], q_s.at[it, 0])
        wait_bytes(sq_b.at[it, pl.ds(0, nw - 1)], q_s.at[it, 1])
    for store in stores:
        store.wait()


def per_device(object_slices, probe, patterns, offsets, owner):
    nslice, _, rows, cols = object_slices.shape
    bands = patterns.shape[0]
    npos, ntile = lax.axis_size("pos"), lax.axis_size("tile")
    nw = 8 if npos % 8 == 0 else 2
    ng = npos // nw * ntile
    chunk = 2 * W // ng
    grown = cols + 2 * M
    cells = float(nslice * 2 * rows * cols * npos * ntile)
    dft, spread = tables()
    vmem, dma = pltpu.VMEM, pltpu.SemaphoreType.DMA
    any_space = pl.BlockSpec(memory_space=pl.ANY)
    smem_space = pl.BlockSpec(memory_space=pltpu.SMEM)
    scratch = [
        pltpu.SMEM((2, bands, 2), jnp.int32),
        pltpu.SMEM((2, bands), jnp.int32),
        vmem((4, M, grown), F32),
        vmem((4, M, grown), F32),
        vmem((4, M, grown), BF16),
        vmem((ITERS, 3, MOST, 4, M, W), BF16),
        vmem((ITERS, 2, MOST, 4, M, W), BF16),
        vmem((ITERS, 2, MOST, 4, M, W), BF16),
        vmem((ITERS, 3, MOST, 4, M, W), BF16),
        vmem((ITERS, 2, 4, M, W), BF16),
        vmem((ITERS, 2, 4, M, W), BF16),
        vmem((2, W, W), F32),
        vmem((bands, W, W), F32),
        vmem((2, 2 * W, 2 * W), BF16),
        vmem((2, W, W), F32),
        vmem((3 * MOST * W, grown), BF16),
        vmem((MOST, W, 3 * M), BF16),
        vmem((MOST, 3 * M, W), BF16),
        vmem((MOST, 4, W, W), F32),
        vmem((MOST, W, 2 * W), BF16),
        vmem((MOST, 2 * W, W), BF16),
        vmem((MOST, 2, W, W), F32),
        vmem((2 * W, W), F32),
        vmem((ITERS, ng, chunk, W), BF16),
        vmem((ITERS, ng, chunk, W), BF16),
        vmem((ITERS, chunk, W), BF16),
        vmem((ITERS, nw, chunk, W), BF16),
        vmem((ITERS, chunk, W), BF16),
        vmem((ITERS, ng, chunk, W), BF16),
        vmem((ITERS, ng, 8, M), F32),
        vmem((ITERS, nw, 8, M), F32),
        vmem((ITERS, 8, M), F32),
        vmem((ITERS, 8, M), F32),
        dma((5,)),
        dma((4,)), dma((4,)),
        dma((2,)), dma((2,)),
        dma((ITERS, 2)), dma((ITERS, 2)),
        dma((ITERS, 2)), dma((ITERS, 2)),
        dma((ITERS, 2)), dma((ITERS, 2)),
        dma((ITERS, 3)), dma((ITERS, 3)),
        dma((ITERS, 2)), dma((ITERS, 2)),
    ]
    field, current = pl.pallas_call(
        functools.partial(body, (npos, ntile, nw, bands, cols, cells)),
        out_shape=(
            jax.ShapeDtypeStruct((4, rows, cols), F32),
            jax.ShapeDtypeStruct((2, W, W), F32),
        ),
        in_specs=[smem_space] * 2 + [any_space] * 5,
        out_specs=(any_space, any_space),
        scratch_shapes=scratch,
        compiler_params=pltpu.CompilerParams(
            collective_id=0, has_side_effects=True, vmem_limit_bytes=56 * 1024 * 1024
        ),
    )(
        offsets,
        owner,
        object_slices.reshape(4, rows, cols),
        probe,
        patterns,
        jnp.asarray(dft),
        jnp.asarray(spread),
    )
    return field.reshape(nslice, 2, rows, cols), current


def solution(mesh):
    return jax.shard_map(
        per_device,
        mesh=mesh,
        in_specs=(
            P(None, None, "pos", "tile"),
            P(),
            P("pos", None, None),
            P("pos", None),
            P("pos"),
        ),
        out_specs=(P(None, None, "pos", "tile"), P()),
        check_vma=False,
    )
```

time: 776 us -> 116 us (0.15)
  waiting for transfers between devices: 344 us -> 0 us
  blocking collectives: 138 us -> 0 us
  Pallas kernels: 0 us -> 109 us
  local copies, waits for them, and re-layouts: 92.8 us -> 5.35 us
  matrix products: 61.1 us -> 0 us
  other arithmetic: 55 us -> 0 us
  starting transfers between devices: 46.5 us -> 0 us
  between operations: 18.2 us -> 0.65 us
  loops' own time: 15.7 us -> 0 us
    psum x2 -> x0, waiting for transfers between devices: 258 us -> none  [per_device(): lax.psum((local_probe, jnp.sum(block_grad * block_grad)), ('pos', 'tile'))]
    psum x2 -> x0, blocking collectives: 138 us -> none  [per_device(): lax.psum((local_probe, jnp.sum(block_grad * block_grad)), ('pos', 'tile'))]
    pallas_call x0 -> x1, Pallas kernels: none -> 109 us  [per_device(): pl.pallas_call(functools.partial(body, (npos, ntile, nw, bands, cols, cel...]
    ppermute x16 -> x0, waiting for transfers between devices: 85.6 us -> none  [the longest x8 60.2 us: from_behind(): return lax.ppermute(block, axis, route)]
    dot_general x48 -> x0, matrix products: 61.1 us -> none  [the longest x12 15.7 us: section(): jnp.einsum('scjk,kl->scjl', field, cosine, preferred_element_type=jnp.flo...]
    dynamic_update_slice x4 -> x0, local copies, waits for them, and re-layouts: 46.8 us -> none  [add_one(): return lax.dynamic_update_slice(total, before + slice_grads[k], start)]
    ppermute x16 -> x0, starting transfers between devices: 46.4 us -> none  [the longest x8 26.1 us: from_behind(): return lax.ppermute(block, axis, route)]
    add x13 -> x0, other arithmetic: 18.4 us -> none  [the longest x4 7.85 us: add_one(): return lax.dynamic_update_slice(total, before + slice_grads[k], start)]
  transfers between devices with their start and end apart: 18 -> 0, of which waited for: 14 -> 0; matrix products, arithmetic and copies ran while one was open for 2% -> 0% of each run, Pallas kernels for 0% -> 0%
where the time goes in v1:
time: 116 us; the launch traced here: 115 us
  Pallas kernels  109 us (94%)
  local copies, waits for them, and re-layouts  5.35 us (5%)
    pallas_call x1, Pallas kernels, per_device(): pl.pallas_call(functools.partial(body, (npos, ntile, nw, bands, cols, cel...  109 us
    unnamed x5, local copies, waits for them, and re-layouts  5.35 us

profile of v1, /device:TPU:1, one launch (start us, length us, event | category | flops | bytes accessed | tf_op | source)
XLA Modules:
  0.0 115.5 jit_solution(10318209958858072538)
XLA Ops:
  0.6 1.3 %copy.9.refs_0_ = s32[4,2]{1,0:T(4,128)} copy(s32[4,2]{0,1:T(2,128)} %param.10) | data formatting | bytes 64 | tf_op args[3]
  2.0 109.5 %shard_map.86 = (f32[4,128,1024]{2,1,0:T(8,128)}, f32[2,256,256]{2,1,0:T(8,128)}) custom-call(s32[4,2]{1,0:T(4,128)} %copy.9.refs_0_, s32[4]{0:T(128)} %refs_1_.1, f32[4,128,1024]{2,1,0:T(8,128)} %bitcast.2, f32[2,256,256]{2,1,0:T(8,128)} %refs_3_.1, f32[4,256,256]{2,1,0:T(8,128)} %refs_4_.1, bf16[2,512,512]{2,1,0:T(8,128)(2,1)} %constant.4.clone.refs_5_, ...), custom_call_target="tpu_custom_call" | custom-call | tf_op jit(solution)/shard_map/pallas_call | solution.py:401
  111.5 0.0 copy-start
  111.5 3.2 %copy.12 = f32[2,2,128,1024]{3,2,1,0:T(8,128)} copy(f32[2,2,128,1024]{3,2,1,0:T(8,128)} %bitcast.3) | data formatting | bytes 4194304
  114.7 0.0 copy-done
  114.7 0.8 copy.13
Async XLA Ops:
  111.5 3.2 %copy-start = (f32[2,256,256]{2,1,0:T(8,128)S(1)}, f32[2,256,256]{2,1,0:T(8,128)}, u32[]{:S(2)}) copy-start(f32[2,256,256]{2,1,0:T(8,128)} %get-tuple-element.9) | copy-start | bytes 1572868

commit v2 on v1

v2 whole, which is shorter than its diff:
```python
import functools
import math

import jax
import jax.numpy as jnp
import numpy as np
from jax import lax
from jax.experimental import pallas as pl
from jax.experimental.pallas import tpu as pltpu
from jax.sharding import PartitionSpec as P

ITERS = 2
MOST = 2
FRESNEL = 0.05
ETA_OBJECT = 0.5
ETA_PROBE = 0.5
W = 256
M = 128
MESH = pl.DeviceIdType.MESH
F32 = jnp.float32
BF16 = jnp.bfloat16


def tables():
    indices = np.arange(W)
    angles = (indices[:, None] * indices[None, :] % W) * (2.0 * math.pi / W)
    cosine = np.cos(angles) / math.sqrt(W)
    sine = np.sin(angles) / math.sqrt(W)
    ahead = np.block([[cosine, -sine], [sine, cosine]])
    behind = np.block([[cosine, sine], [-sine, cosine]])
    dft = np.stack([ahead, behind]).astype(np.float32).astype(jnp.bfloat16)
    frequency = ((indices + W // 2) % W - W // 2).astype(np.float32)
    phases = -math.pi * FRESNEL / W * (frequency[:, None] ** 2 + frequency[None, :] ** 2)
    spread = np.stack([np.cos(phases), np.sin(phases)]).astype(np.float32)
    return dft, spread


def slot_info(owner_of, offset_of, bands, tile):
    zero = jnp.int32(0)
    found = zero
    slots = [[zero, zero, zero, zero] for _ in range(MOST)]
    for n in range(bands):
        live = owner_of(n) == tile
        row, col = offset_of(n, 0) + M, offset_of(n, 1) + M
        for k in range(MOST):
            here = jnp.logical_and(live, found == k)
            slots[k] = [
                jnp.where(here, new, old)
                for new, old in zip((row, col, jnp.int32(n), jnp.int32(1)), slots[k])
            ]
        found = found + live.astype(jnp.int32)
    return slots


def one_hot(rows, cols, shift):
    row = lax.broadcasted_iota(jnp.int32, (rows, cols), 0)
    col = lax.broadcasted_iota(jnp.int32, (rows, cols), 1)
    return (row == col + shift).astype(F32).astype(BF16)


def dot(a, b):
    return jnp.dot(a, b, preferred_element_type=F32)


def body(sizes, *refs):
    (npos, ntile, nw, bands, block_cols, cells) = sizes
    (off_in, own_in, obj, probe_in, pats_in, tab_in, spread_in, obj_out, probe_out) = refs[:9]
    (
        off, own, off_nb, own_nb, fld, acc, low, steps, parts, halo_send, fold_send, contrib, edge_send, edge_recv,
        probe, pats, wanted, tab, spread, place, rows_in, rows_out, patch, x, mid, psi1, pg,
        rs1_send, rs1, rs2_send, rs2, ag_send, ag, sq_a, sq_b, sq_sa, sq_sb,
        local_sem, info_s, info_r, col_s, col_r, halo_s, halo_r, fold_s, fold_r, edge_s, edge_r,
        p_s, p_r, q_s, q_r,
    ) = refs[9:]
    grown = block_cols + 2 * M
    nx = npos // nw
    ng = nx * ntile
    chunk = 2 * W // ng
    p = lax.axis_index("pos")
    t = lax.axis_index("tile")
    xi, wi = p // nw, p % nw
    me_g = xi * ntile + t

    up = {"pos": lax.rem(p + npos - 1, npos)}
    down = {"pos": lax.rem(p + 1, npos)}
    left = {"tile": lax.rem(t + ntile - 1, ntile)}
    right = {"tile": lax.rem(t + 1, ntile)}

    def g_peer(j):
        return {
            "pos": lax.rem(xi + j // ntile, nx) * nw + wi,
            "tile": lax.rem(t + j % ntile, ntile),
        }

    def g_index(j):
        return lax.rem(xi + j // ntile, nx) * ntile + lax.rem(t + j % ntile, ntile)

    def w_peer(j):
        return {"pos": xi * nw + lax.rem(wi + j, nw)}

    def remote(src, dst, send, recv, where):
        return pltpu.make_async_remote_copy(
            src_ref=src, dst_ref=dst, send_sem=send, recv_sem=recv, device_id=where, device_id_type=MESH
        )

    def wait_bytes(ref, sem):
        pltpu.make_async_copy(ref, ref, sem).wait()

    loads = [
        pltpu.make_async_copy(off_in, off, local_sem.at[0]),
        pltpu.make_async_copy(own_in, own, local_sem.at[1]),
        pltpu.make_async_copy(obj, fld, local_sem.at[2]),
        pltpu.make_async_copy(pats_in, pats, local_sem.at[3]),
        pltpu.make_async_copy(probe_in, probe, local_sem.at[4]),
        pltpu.make_async_copy(tab_in, tab, local_sem.at[5]),
        pltpu.make_async_copy(spread_in, spread, local_sem.at[6]),
    ]
    for load in loads:
        load.start()

    barrier = pltpu.get_barrier_semaphore()
    friends = [up, down, left, right]
    friends += [g_peer(j) for j in range(1, ng)]
    friends += [w_peer(j) for j in range(1, nw)]
    for friend in friends:
        pl.semaphore_signal(barrier, inc=1, device_id=friend, device_id_type=MESH)
    for load in loads[:3]:
        load.wait()
    low[:, :, pl.ds(M, block_cols)] = fld[...].astype(BF16)
    pl.semaphore_wait(barrier, len(friends))

    info = [
        remote(off, off_nb.at[0], info_s.at[0], info_r.at[0], down),
        remote(own, own_nb.at[0], info_s.at[1], info_r.at[1], down),
        remote(off, off_nb.at[1], info_s.at[2], info_r.at[2], up),
        remote(own, own_nb.at[1], info_s.at[3], info_r.at[3], up),
    ]
    for copy in info:
        copy.start()
    cols = []
    for s in range(2):
        rows = pl.ds(2 * s, 2)
        cols.append([
            remote(
                low.at[rows, :, pl.ds(block_cols, M)], low.at[rows, :, pl.ds(0, M)],
                col_s.at[s, 0], col_r.at[s, 0], right,
            ),
            remote(
                low.at[rows, :, pl.ds(M, M)], low.at[rows, :, pl.ds(M + block_cols, M)],
                col_s.at[s, 1], col_r.at[s, 1], left,
            ),
        ])
        for copy in cols[s]:
            copy.start()
    sends = info + cols[0] + cols[1]

    def build_place(k, slot):
        place[pl.ds(k * W, W), :] = (
            lax.broadcasted_iota(jnp.int32, (W, grown), 1)
            == lax.broadcasted_iota(jnp.int32, (W, grown), 0) + slot[1]
        ).astype(F32).astype(BF16)

    mine = slot_info(lambda n: own[n], lambda n, i: off[n, i], bands, t)
    for k in range(MOST):
        rows_in[k] = (
            lax.broadcasted_iota(jnp.int32, (W, 3 * M), 1)
            == lax.broadcasted_iota(jnp.int32, (W, 3 * M), 0) + mine[k][0]
        ).astype(F32).astype(BF16)
        rows_out[k] = one_hot(3 * M, W, mine[k][0])
        build_place(MOST + k, mine[k])
    for copy in info:
        copy.wait_recv()
    above = slot_info(lambda n: own_nb[0, n], lambda n, i: off_nb[0, n, i], bands, t)
    below = slot_info(lambda n: own_nb[1, n], lambda n, i: off_nb[1, n, i], bands, t)
    for k in range(MOST):
        build_place(k, above[k])
        build_place(2 * MOST + k, below[k])

    def chosen(source, s, group):
        return lax.dot_general(
            source[pl.ds(2 * s, 2)].reshape(2 * M, grown),
            place[pl.ds(group * MOST * W, MOST * W), :],
            (((1,), (1,)), ((), ())),
            preferred_element_type=F32,
        ).astype(BF16)

    def start_halo(h, s, source):
        copies = []
        for way, (group, part, where) in enumerate(((0, 2, up), (2, 0, down))):
            columns = chosen(source, s, group)
            for k in range(MOST):
                halo_send[h, way, s, k] = columns[:, k * W : (k + 1) * W].reshape(2, M, W)
            copy = remote(
                halo_send.at[h, way, s], parts.at[h, part, s], halo_s.at[h, s, way], halo_r.at[h, s, way], where
            )
            copy.start()
            copies.append(copy)
        return copies

    def own_columns(h, s, source):
        columns = chosen(source, s, 1)
        for k in range(MOST):
            parts[h, 1, s, k] = columns[:, k * W : (k + 1) * W].reshape(2, M, W)

    def window(h, s, k, c):
        stack = jnp.concatenate([parts[h, 0, s, k, c], parts[h, 1, s, k, c], parts[h, 2, s, k, c]], axis=0)
        return dot(rows_in[k], stack)

    halo = []
    for s in range(2):
        for copy in cols[s]:
            copy.wait_recv()
        halo.append(start_halo(0, s, low))
    for s in range(2):
        own_columns(0, s, low)
    for load in loads[3:]:
        load.wait()
    for k in range(MOST):
        found = pats[0]
        for n in range(1, bands):
            found = jnp.where(mine[k][2] == n, pats[n], found)
        wanted[k] = found

    def transform(k, way):
        half = dot(x[k], tab[way]).astype(BF16)
        mid[k, pl.ds(0, W)] = half[:, :W]
        mid[k, pl.ds(W, W)] = half[:, W:]
        both = dot(tab[1 - way], mid[k])
        return both[:W], both[W:]

    def put(k, re, im):
        x[k, :, pl.ds(0, W)] = re.astype(BF16)
        x[k, :, pl.ds(W, W)] = im.astype(BF16)

    for it in range(ITERS):

        def fold_out(k, s, c, value):
            rows = dot(rows_out[k], value.astype(BF16)).astype(BF16)
            fold_send[it, 0, s, k, c] = rows[:M]
            contrib[it, 1, s, k, c] = rows[M : 2 * M]
            fold_send[it, 1, s, k, c] = rows[2 * M :]

        def start_fold(s):
            copies = [
                remote(
                    fold_send.at[it, 0, s], contrib.at[it, 2, s], fold_s.at[it, s, 0], fold_r.at[it, s, 0], up
                ),
                remote(
                    fold_send.at[it, 1, s], contrib.at[it, 0, s], fold_s.at[it, s, 1], fold_r.at[it, s, 1], down
                ),
            ]
            for copy in copies:
                copy.start()
            return copies

        def sum_columns(terms, s, start):
            acc[pl.ds(2 * s, 2), :, pl.ds(start, W)] = dot(terms, place[:, pl.ds(start, W)]).reshape(2, M, W)

        def sum_slice(s):
            terms = jnp.concatenate(
                [contrib[it, g, s, k].reshape(2 * M, W) for g in range(3) for k in range(MOST)], axis=1
            )
            copies = []
            for way, (start, where) in enumerate(((0, left), (grown - W, right))):
                sum_columns(terms, s, start)
                edge_send[it, way, s] = acc[pl.ds(2 * s, 2), :, pl.ds(start, W)].astype(BF16)
                copy = remote(
                    edge_send.at[it, way, s], edge_recv.at[it, 1 - way, s],
                    edge_s.at[it, s, way], edge_r.at[it, s, way], where,
                )
                copy.start()
                copies.append(copy)
            for start in range(W, grown - W, W):
                sum_columns(terms, s, start)
            return copies

        def add_edges(s, copies):
            for copy in copies:
                copy.wait_recv()
            rows = pl.ds(2 * s, 2)
            acc[rows, :, pl.ds(0, W)] = acc[rows, :, pl.ds(0, W)] + edge_recv[it, 0, s].astype(F32)
            acc[rows, :, pl.ds(grown - W, W)] = acc[rows, :, pl.ds(grown - W, W)] + edge_recv[it, 1, s].astype(F32)

        def squares(s):
            inner = acc[pl.ds(2 * s, 2), :, pl.ds(M, block_cols)].reshape(2 * M // 8, 8, block_cols)
            summed = jnp.sum(inner * inner, axis=0)
            total = summed[:, :M]
            for i in range(1, block_cols // M):
                total = total + summed[:, i * M : (i + 1) * M]
            return total

        for copy in halo[0]:
            copy.wait_recv()
        for k in range(MOST):
            for c in range(2):
                found = window(it, 0, k, c)
                patch[k, c] = found if it == 0 else patch[k, c] - scale * found
            re = probe[0] * patch[k, 0] - probe[1] * patch[k, 1]
            im = probe[0] * patch[k, 1] + probe[1] * patch[k, 0]
            put(k, re, im)
        for k in range(MOST):
            a, b = transform(k, 0)
            put(k, spread[0] * a - spread[1] * b, spread[0] * b + spread[1] * a)
        for copy in halo[1]:
            copy.wait_recv()
        for k in range(MOST):
            for c in range(2):
                found = window(it, 1, k, c)
                patch[k, 2 + c] = found if it == 0 else patch[k, 2 + c] - scale * found
        if it > 0:
            fld[...] = fld[...] - scale * acc[:, :, pl.ds(M, block_cols)]
        for k in range(MOST):
            a, b = transform(k, 1)
            psi1[k, 0] = a
            psi1[k, 1] = b
            put(k, a * patch[k, 2] - b * patch[k, 3], a * patch[k, 3] + b * patch[k, 2])
        for k in range(MOST):
            a, b = transform(k, 0)
            misfit = jnp.where(mine[k][3] > 0, a * a + b * b - wanted[k], 0.0)
            put(k, misfit * a, misfit * b)

        for k in range(MOST):
            a, b = transform(k, 1)
            put(k, patch[k, 2] * a + patch[k, 3] * b, patch[k, 2] * b - patch[k, 3] * a)
            fold_out(k, 1, 0, psi1[k, 0] * a + psi1[k, 1] * b)
            fold_out(k, 1, 1, psi1[k, 0] * b - psi1[k, 1] * a)
        fold1 = start_fold(1)
        for k in range(MOST):
            a, b = transform(k, 0)
            put(k, spread[0] * a + spread[1] * b, spread[0] * b - spread[1] * a)
        for k in range(MOST):
            a, b = transform(k, 1)
            fold_out(k, 0, 0, probe[0] * a + probe[1] * b)
            fold_out(k, 0, 1, probe[0] * b - probe[1] * a)
            re = patch[k, 0] * a + patch[k, 1] * b
            im = patch[k, 0] * b - patch[k, 1] * a
            if k == 0:
                pg[pl.ds(0, W)] = re
                pg[pl.ds(W, W)] = im
            else:
                pg[pl.ds(0, W)] = pg[pl.ds(0, W)] + re
                pg[pl.ds(W, W)] = pg[pl.ds(W, W)] + im
        fold0 = start_fold(0)

        rs1_send[it] = pg[...].astype(BF16).reshape(ng, chunk, W)
        for j in range(1, ng):
            remote(
                rs1_send.at[it, g_index(j)], rs1.at[it, me_g], p_s.at[it, 0], p_r.at[it, 0], g_peer(j)
            ).start()
        rs1[it, me_g] = rs1_send[it, me_g]

        for copy in fold1:
            copy.wait_recv()
        edge1 = sum_slice(1)
        for copy in fold0:
            copy.wait_recv()
        edge0 = sum_slice(0)

        wait_bytes(rs1.at[it, pl.ds(0, ng - 1)], p_r.at[it, 0])
        rs2_send[it] = jnp.sum(rs1[it].astype(F32), axis=0).astype(BF16)
        for j in range(1, nw):
            remote(rs2_send.at[it], rs2.at[it, wi], p_s.at[it, 1], p_r.at[it, 1], w_peer(j)).start()
        rs2[it, wi] = rs2_send[it]

        more = it + 1 < ITERS
        sends += fold0 + fold1 + edge0 + edge1 + halo[0] + halo[1]
        halo = [None, None]
        for s, copies in ((1, edge1), (0, edge0)):
            add_edges(s, copies)
            if more:
                steps[pl.ds(2 * s, 2)] = acc[pl.ds(2 * s, 2)].astype(BF16)
                halo[s] = start_halo(it + 1, s, steps)
        sq_sa[it] = squares(0) + squares(1)
        for j in range(1, ng):
            remote(sq_sa.at[it], sq_a.at[it, me_g], q_s.at[it, 0], q_r.at[it, 0], g_peer(j)).start()
        sq_a[it, me_g] = sq_sa[it]

        wait_bytes(rs2.at[it, pl.ds(0, nw - 1)], p_r.at[it, 1])
        ag_send[it] = jnp.sum(rs2[it].astype(F32), axis=0).astype(BF16)
        for j in range(1, ng):
            remote(ag_send.at[it], ag.at[it, me_g], p_s.at[it, 2], p_r.at[it, 2], g_peer(j)).start()
        ag[it, me_g] = ag_send[it]

        if more:
            for s in range(2):
                own_columns(it + 1, s, steps)

        wait_bytes(sq_a.at[it, pl.ds(0, ng - 1)], q_r.at[it, 0])
        sq_sb[it] = jnp.sum(sq_a[it], axis=0)
        for j in range(1, nw):
            remote(sq_sb.at[it], sq_b.at[it, wi], q_s.at[it, 1], q_r.at[it, 1], w_peer(j)).start()
        sq_b[it, wi] = sq_sb[it]

        wait_bytes(ag.at[it, pl.ds(0, ng - 1)], p_r.at[it, 2])
        grad = ag[it].astype(F32).reshape(2, W, W)
        mean = jnp.sum(grad * grad) / float(2 * W * W)
        probe[...] = probe[...] - ETA_PROBE * lax.rsqrt(mean + 1e-06) * grad

        wait_bytes(sq_b.at[it, pl.ds(0, nw - 1)], q_r.at[it, 1])
        mean = jnp.sum(jnp.sum(sq_b[it], axis=0)) / cells
        scale = ETA_OBJECT * lax.rsqrt(mean + 1e-06)

    stores = [pltpu.make_async_copy(probe, probe_out, local_sem.at[4])]
    stores[0].start()
    for c in range(4):
        fld[c] = fld[c] - scale * acc[c, :, pl.ds(M, block_cols)]
        store = pltpu.make_async_copy(fld.at[c], obj_out.at[c], local_sem.at[c])
        store.start()
        stores.append(store)
    for copy in sends:
        copy.wait_send()
    for it in range(ITERS):
        wait_bytes(rs1_send.at[it, pl.ds(0, ng - 1)], p_s.at[it, 0])
        wait_bytes(rs2.at[it, pl.ds(0, nw - 1)], p_s.at[it, 1])
        wait_bytes(ag.at[it, pl.ds(0, ng - 1)], p_s.at[it, 2])
        wait_bytes(sq_a.at[it, pl.ds(0, ng - 1)], q_s.at[it, 0])
        wait_bytes(sq_b.at[it, pl.ds(0, nw - 1)], q_s.at[it, 1])
    for store in stores:
        store.wait()


def per_device(object_slices, probe, patterns, offsets, owner):
    nslice, _, rows, cols = object_slices.shape
    bands = patterns.shape[0]
    npos, ntile = lax.axis_size("pos"), lax.axis_size("tile")
    nw = 8 if npos % 8 == 0 else 2
    ng = npos // nw * ntile
    chunk = 2 * W // ng
    grown = cols + 2 * M
    cells = float(nslice * 2 * rows * cols * npos * ntile)
    dft, spread = tables()
    vmem, dma = pltpu.VMEM, pltpu.SemaphoreType.DMA
    any_space = pl.BlockSpec(memory_space=pl.ANY)
    scratch = [
        pltpu.SMEM((bands, 2), jnp.int32),
        pltpu.SMEM((bands,), jnp.int32),
        pltpu.SMEM((2, bands, 2), jnp.int32),
        pltpu.SMEM((2, bands), jnp.int32),
        vmem((4, M, cols), F32),
        vmem((4, M, grown), F32),
        vmem((4, M, grown), BF16),
        vmem((4, M, grown), BF16),
        vmem((ITERS, 3, 2, MOST, 2, M, W), BF16),
        vmem((ITERS, 2, 2, MOST, 2, M, W), BF16),
        vmem((ITERS, 2, 2, MOST, 2, M, W), BF16),
        vmem((ITERS, 3, 2, MOST, 2, M, W), BF16),
        vmem((ITERS, 2, 2, 2, M, W), BF16),
        vmem((ITERS, 2, 2, 2, M, W), BF16),
        vmem((2, W, W), F32),
        vmem((bands, W, W), F32),
        vmem((MOST, W, W), F32),
        vmem((2, 2 * W, 2 * W), BF16),
        vmem((2, W, W), F32),
        vmem((3 * MOST * W, grown), BF16),
        vmem((MOST, W, 3 * M), BF16),
        vmem((MOST, 3 * M, W), BF16),
        vmem((MOST, 4, W, W), F32),
        vmem((MOST, W, 2 * W), BF16),
        vmem((MOST, 2 * W, W), BF16),
        vmem((MOST, 2, W, W), F32),
        vmem((2 * W, W), F32),
        vmem((ITERS, ng, chunk, W), BF16),
        vmem((ITERS, ng, chunk, W), BF16),
        vmem((ITERS, chunk, W), BF16),
        vmem((ITERS, nw, chunk, W), BF16),
        vmem((ITERS, chunk, W), BF16),
        vmem((ITERS, ng, chunk, W), BF16),
        vmem((ITERS, ng, 8, M), F32),
        vmem((ITERS, nw, 8, M), F32),
        vmem((ITERS, 8, M), F32),
        vmem((ITERS, 8, M), F32),
        dma((7,)),
        dma((4,)), dma((4,)),
        dma((2, 2)), dma((2, 2)),
        dma((ITERS, 2, 2)), dma((ITERS, 2, 2)),
        dma((ITERS, 2, 2)), dma((ITERS, 2, 2)),
        dma((ITERS, 2, 2)), dma((ITERS, 2, 2)),
        dma((ITERS, 3)), dma((ITERS, 3)),
        dma((ITERS, 2)), dma((ITERS, 2)),
    ]
    field, current = pl.pallas_call(
        functools.partial(body, (npos, ntile, nw, bands, cols, cells)),
        out_shape=(
            jax.ShapeDtypeStruct((4, rows, cols), F32),
            jax.ShapeDtypeStruct((2, W, W), F32),
        ),
        in_specs=[any_space] * 7,
        out_specs=(any_space, any_space),
        scratch_shapes=scratch,
        compiler_params=pltpu.CompilerParams(
            collective_id=0, has_side_effects=True, vmem_limit_bytes=48 * 1024 * 1024
        ),
    )(
        offsets,
        owner,
        object_slices.reshape(4, rows, cols),
        probe,
        patterns,
        jnp.asarray(dft),
        jnp.asarray(spread),
    )
    return field.reshape(nslice, 2, rows, cols), current


def solution(mesh):
    return jax.shard_map(
        per_device,
        mesh=mesh,
        in_specs=(
            P(None, None, "pos", "tile"),
            P(),
            P("pos", None, None),
            P("pos", None),
            P("pos"),
        ),
        out_specs=(P(None, None, "pos", "tile"), P()),
        check_vma=False,
    )
```

time: 116 us -> 94.1 us (0.81)
  Pallas kernels: 109 us -> 85 us
  local copies, waits for them, and re-layouts: 5.35 us -> 8.07 us
    pallas_call x1, Pallas kernels: 109 us -> 85 us  [per_device(): pl.pallas_call(functools.partial(body, (npos, ntile, nw, bands, cols, cel...]
    unnamed x5 -> x13, local copies, waits for them, and re-layouts: 5.35 us -> 8.07 us
where the time goes in v2:
time: 94.1 us; the launch traced here: 93.7 us
  Pallas kernels  85 us (90%)
  local copies, waits for them, and re-layouts  8.07 us (9%)
    pallas_call x1, Pallas kernels, per_device(): pl.pallas_call(functools.partial(body, (npos, ntile, nw, bands, cols, cel...  85 us
    unnamed x13, local copies, waits for them, and re-layouts  8.07 us

profile of v2, /device:TPU:1, one launch (start us, length us, event | category | flops | bytes accessed | tf_op | source)
XLA Modules:
  0.0 93.7 jit_solution(3940199300598221539)
XLA Ops:
  0.6 0.8 copy.9.refs_0_
  1.4 0.0 copy-start
  1.4 1.2 %copy-done = f32[4,256,256]{2,1,0:T(8,128)S(1)} copy-done((f32[4,256,256]{2,1,0:T(8,128)S(1)}, f32[4,256,256]{2,1,0:T(8,128)}, u32[]{:S(2)}) %copy-start) | copy-done | bytes 1048600
  2.6 0.0 copy-start.1
  2.6 1.2 %copy-done.1 = bf16[2,512,512]{2,1,0:T(8,128)(2,1)S(1)} copy-done((bf16[2,512,512]{2,1,0:T(8,128)(2,1)S(1)}, bf16[2,512,512]{2,1,0:T(8,128)(2,1)}, u32[]{:S(2)}) %copy-start.1) | copy-done | bytes 1048600
  3.8 0.0 copy-start.2
  3.8 1.0 %copy-done.2 = f32[2,256,256]{2,1,0:T(8,128)S(1)} copy-done((f32[2,256,256]{2,1,0:T(8,128)S(1)}, f32[2,256,256]{2,1,0:T(8,128)}, u32[]{:S(2)}) %copy-start.2) | copy-done | bytes 524312
  4.9 0.0 copy-start.3
  4.9 1.0 %copy-done.3 = f32[2,256,256]{2,1,0:T(8,128)S(1)} copy-done((f32[2,256,256]{2,1,0:T(8,128)S(1)}, f32[2,256,256]{2,1,0:T(8,128)}, u32[]{:S(2)}) %copy-start.3) | copy-done | bytes 524312
  5.9 0.0 copy-start.4
  5.9 0.7 copy-done.4
  6.6 85.0 %shard_map.86 = (f32[4,128,1024]{2,1,0:T(8,128)S(1)}, f32[2,256,256]{2,1,0:T(8,128)S(1)}) custom-call(s32[4,2]{1,0:T(4,128)S(1)} %copy.9.refs_0_, s32[4]{0:T(128)S(1)} %copy-done.4, f32[4,128,1024]{2,1,0:T(8,128)} %bitcast.3, f32[2,256,256]{2,1,0:T(8,128)S(1)} %copy-done.2, f32[4,256,256]{2,1,0:T(8,128)S(1)} %copy-done, bf16[2,512,512]{2,1,0:T(8,128)(2,1)S(1)} %copy-done.1, ...), custom_call_target="tpu_custom_call" | custom-call | tf_op jit(solution)/shard_map/pallas_call | solution.py:481
  91.6 1.3 %copy.12 = f32[2,2,128,1024]{3,2,1,0:T(8,128)} copy(f32[2,2,128,1024]{3,2,1,0:T(8,128)S(1)} %bitcast.2) | data formatting | bytes 4194304
  92.9 0.8 copy.13
Async XLA Ops:
  1.4 1.2 %copy-start = (f32[4,256,256]{2,1,0:T(8,128)S(1)}, f32[4,256,256]{2,1,0:T(8,128)}, u32[]{:S(2)}) copy-start(f32[4,256,256]{2,1,0:T(8,128)} %refs_4_.1) | copy-start | bytes 3145732
  2.6 1.2 %copy-start.1 = (bf16[2,512,512]{2,1,0:T(8,128)(2,1)S(1)}, bf16[2,512,512]{2,1,0:T(8,128)(2,1)}, u32[]{:S(2)}) copy-start(bf16[2,512,512]{2,1,0:T(8,128)(2,1)} %constant.4.clone.refs_5_) | copy-start | bytes 3145732
  3.8 1.0 %copy-start.2 = (f32[2,256,256]{2,1,0:T(8,128)S(1)}, f32[2,256,256]{2,1,0:T(8,128)}, u32[]{:S(2)}) copy-start(f32[2,256,256]{2,1,0:T(8,128)} %refs_3_.1) | copy-start | bytes 1572868
  4.9 1.0 %copy-start.3 = (f32[2,256,256]{2,1,0:T(8,128)S(1)}, f32[2,256,256]{2,1,0:T(8,128)}, u32[]{:S(2)}) copy-start(f32[2,256,256]{2,1,0:T(8,128)} %constant.5.clone.refs_6_) | copy-start | bytes 1572868
  5.9 0.7 copy-start.4

commit v3 on v2

--- a/solution.py
+++ b/solution.py
@@ -66,13 +66,15 @@
     (npos, ntile, nw, bands, block_cols, cells) = sizes
     (off_in, own_in, obj, probe_in, pats_in, tab_in, spread_in, obj_out, probe_out) = refs[:9]
     (
-        off, own, off_nb, own_nb, fld, acc, low, steps, parts, halo_send, fold_send, contrib, edge_send, edge_recv,
-        probe, pats, wanted, tab, spread, place, rows_in, rows_out, patch, x, mid, psi1, pg,
+        off, own, off_nb, own_nb, fld, acc, low0, low1, steps, parts, halo_send, fold_send, contrib, edge_send, edge_recv,
+        probe, pats, wanted, tab, spread, sel, place, rows_in, rows_out, patch, x, mid, psi1, pg,
         rs1_send, rs1, rs2_send, rs2, ag_send, ag, sq_a, sq_b, sq_sa, sq_sb,
         local_sem, info_s, info_r, col_s, col_r, halo_s, halo_r, fold_s, fold_r, edge_s, edge_r,
         p_s, p_r, q_s, q_r,
     ) = refs[9:]
-    grown = block_cols + 2 * M
+    inner = block_cols // M
+    low = (low0, low1)
+    ntiles = inner + 2
     nx = npos // nw
     ng = nx * ntile
     chunk = 2 * W // ng
@@ -126,7 +128,9 @@
         pl.semaphore_signal(barrier, inc=1, device_id=friend, device_id_type=MESH)
     for load in loads[:3]:
         load.wait()
-    low[:, :, pl.ds(M, block_cols)] = fld[...].astype(BF16)
+    for s in range(2):
+        for j in range(inner):
+            low[s][1 + j] = fld[pl.ds(2 * s, 2), :, pl.ds(j * M, M)].reshape(2 * M, M).astype(BF16)
     pl.semaphore_wait(barrier, len(friends))
 
     info = [
@@ -139,57 +143,46 @@
         copy.start()
     cols = []
     for s in range(2):
-        rows = pl.ds(2 * s, 2)
         cols.append([
-            remote(
-                low.at[rows, :, pl.ds(block_cols, M)], low.at[rows, :, pl.ds(0, M)],
-                col_s.at[s, 0], col_r.at[s, 0], right,
-            ),
-            remote(
-                low.at[rows, :, pl.ds(M, M)], low.at[rows, :, pl.ds(M + block_cols, M)],
-                col_s.at[s, 1], col_r.at[s, 1], left,
-            ),
+            remote(low[s].at[inner], low[s].at[0], col_s.at[s, 0], col_r.at[s, 0], right),
+            remote(low[s].at[1], low[s].at[inner + 1], col_s.at[s, 1], col_r.at[s, 1], left),
         ])
         for copy in cols[s]:
             copy.start()
     sends = info + cols[0] + cols[1]
 
-    def build_place(k, slot):
-        place[pl.ds(k * W, W), :] = (
-            lax.broadcasted_iota(jnp.int32, (W, grown), 1)
-            == lax.broadcasted_iota(jnp.int32, (W, grown), 0) + slot[1]
-        ).astype(F32).astype(BF16)
-
-    mine = slot_info(lambda n: own[n], lambda n, i: off[n, i], bands, t)
+    firsts = [None] * (3 * MOST)
+
+    def build_sel(k, slot):
+        firsts[k] = jnp.minimum(slot[1] // M, inner - 1)
+        sel[k] = one_hot(3 * M, W, slot[1] - firsts[k] * M)
+
+    mine = slot_info(lambda n: own[n], lambda n, i: off[i, n], bands, t)
     for k in range(MOST):
+        build_sel(MOST + k, mine[k])
         rows_in[k] = (
             lax.broadcasted_iota(jnp.int32, (W, 3 * M), 1)
             == lax.broadcasted_iota(jnp.int32, (W, 3 * M), 0) + mine[k][0]
         ).astype(F32).astype(BF16)
         rows_out[k] = one_hot(3 * M, W, mine[k][0])
-        build_place(MOST + k, mine[k])
     for copy in info:
         copy.wait_recv()
-    above = slot_info(lambda n: own_nb[0, n], lambda n, i: off_nb[0, n, i], bands, t)
-    below = slot_info(lambda n: own_nb[1, n], lambda n, i: off_nb[1, n, i], bands, t)
+    above = slot_info(lambda n: own_nb[0, n], lambda n, i: off_nb[0, i, n], bands, t)
+    below = slot_info(lambda n: own_nb[1, n], lambda n, i: off_nb[1, i, n], bands, t)
     for k in range(MOST):
-        build_place(k, above[k])
-        build_place(2 * MOST + k, below[k])
-
-    def chosen(source, s, group):
-        return lax.dot_general(
-            source[pl.ds(2 * s, 2)].reshape(2 * M, grown),
-            place[pl.ds(group * MOST * W, MOST * W), :],
-            (((1,), (1,)), ((), ())),
-            preferred_element_type=F32,
-        ).astype(BF16)
+        build_sel(k, above[k])
+        build_sel(2 * MOST + k, below[k])
+
+    def chosen(source, k):
+        first = firsts[k]
+        near = jnp.concatenate([source[first], source[first + 1], source[first + 2]], axis=1)
+        return dot(near, sel[k]).astype(BF16).reshape(2, M, W)
 
     def start_halo(h, s, source):
         copies = []
         for way, (group, part, where) in enumerate(((0, 2, up), (2, 0, down))):
-            columns = chosen(source, s, group)
             for k in range(MOST):
-                halo_send[h, way, s, k] = columns[:, k * W : (k + 1) * W].reshape(2, M, W)
+                halo_send[h, way, s, k] = chosen(source, group * MOST + k)
             copy = remote(
                 halo_send.at[h, way, s], parts.at[h, part, s], halo_s.at[h, s, way], halo_r.at[h, s, way], where
             )
@@ -198,9 +191,8 @@
         return copies
 
     def own_columns(h, s, source):
-        columns = chosen(source, s, 1)
-        for k in range(MOST):
-            parts[h, 1, s, k] = columns[:, k * W : (k + 1) * W].reshape(2, M, W)
+        for k in range(MOST):
+            parts[h, 1, s, k] = chosen(source, MOST + k)
 
     def window(h, s, k, c):
         stack = jnp.concatenate([parts[h, 0, s, k, c], parts[h, 1, s, k, c], parts[h, 2, s, k, c]], axis=0)
@@ -210,9 +202,9 @@
     for s in range(2):
         for copy in cols[s]:
             copy.wait_recv()
-        halo.append(start_halo(0, s, low))
+        halo.append(start_halo(0, s, low[s]))
     for s in range(2):
-        own_columns(0, s, low)
+        own_columns(0, s, low[s])
     for load in loads[3:]:
         load.wait()
     for k in range(MOST):
@@ -220,6 +212,11 @@
         for n in range(1, bands):
             found = jnp.where(mine[k][2] == n, pats[n], found)
         wanted[k] = found
+    for k, slot in enumerate(above + mine + below):
+        place[pl.ds(k * W, W), :] = (
+            lax.broadcasted_iota(jnp.int32, (W, ntiles * M), 1)
+            == lax.broadcasted_iota(jnp.int32, (W, ntiles * M), 0) + slot[1]
+        ).astype(F32).astype(BF16)
 
     def transform(k, way):
         half = dot(x[k], tab[way]).astype(BF16)
@@ -253,41 +250,36 @@
                 copy.start()
             return copies
 
-        def sum_columns(terms, s, start):
-            acc[pl.ds(2 * s, 2), :, pl.ds(start, W)] = dot(terms, place[:, pl.ds(start, W)]).reshape(2, M, W)
-
-        def sum_slice(s):
+        def sum_columns(terms, s, j):
+            both = dot(terms, place[:, pl.ds(j * M, 2 * M)])
+            acc[s, j] = both[:, :M]
+            acc[s, j + 1] = both[:, M:]
+
+        def sum_edges(s):
             terms = jnp.concatenate(
                 [contrib[it, g, s, k].reshape(2 * M, W) for g in range(3) for k in range(MOST)], axis=1
             )
             copies = []
-            for way, (start, where) in enumerate(((0, left), (grown - W, right))):
-                sum_columns(terms, s, start)
-                edge_send[it, way, s] = acc[pl.ds(2 * s, 2), :, pl.ds(start, W)].astype(BF16)
+            for way, (j, where) in enumerate(((0, left), (ntiles - 2, right))):
+                sum_columns(terms, s, j)
+                edge_send[it, way, s] = acc[s, pl.ds(j, 2)].astype(BF16)
                 copy = remote(
                     edge_send.at[it, way, s], edge_recv.at[it, 1 - way, s],
                     edge_s.at[it, s, way], edge_r.at[it, s, way], where,
                 )
                 copy.start()
                 copies.append(copy)
-            for start in range(W, grown - W, W):
-                sum_columns(terms, s, start)
-            return copies
+            return terms, copies
 
         def add_edges(s, copies):
             for copy in copies:
                 copy.wait_recv()
-            rows = pl.ds(2 * s, 2)
-            acc[rows, :, pl.ds(0, W)] = acc[rows, :, pl.ds(0, W)] + edge_recv[it, 0, s].astype(F32)
-            acc[rows, :, pl.ds(grown - W, W)] = acc[rows, :, pl.ds(grown - W, W)] + edge_recv[it, 1, s].astype(F32)
-
-        def squares(s):
-            inner = acc[pl.ds(2 * s, 2), :, pl.ds(M, block_cols)].reshape(2 * M // 8, 8, block_cols)
-            summed = jnp.sum(inner * inner, axis=0)
-            total = summed[:, :M]
-            for i in range(1, block_cols // M):
-                total = total + summed[:, i * M : (i + 1) * M]
-            return total
+            acc[s, pl.ds(0, 2)] = acc[s, pl.ds(0, 2)] + edge_recv[it, 0, s].astype(F32)
+            acc[s, pl.ds(ntiles - 2, 2)] = acc[s, pl.ds(ntiles - 2, 2)] + edge_recv[it, 1, s].astype(F32)
+
+        def squares(s, j, count):
+            values = acc[s, pl.ds(j, count)].reshape(count * 2 * M // 8, 8, M)
+            return jnp.sum(values * values, axis=0)
 
         for copy in halo[0]:
             copy.wait_recv()
@@ -308,7 +300,10 @@
                 found = window(it, 1, k, c)
                 patch[k, 2 + c] = found if it == 0 else patch[k, 2 + c] - scale * found
         if it > 0:
-            fld[...] = fld[...] - scale * acc[:, :, pl.ds(M, block_cols)]
+            for s in range(2):
+                for j in range(inner):
+                    here = (pl.ds(2 * s, 2), slice(None), pl.ds(j * M, M))
+                    fld[here] = fld[here] - scale * acc[s, 1 + j].reshape(2, M, M)
         for k in range(MOST):
             a, b = transform(k, 1)
             psi1[k, 0] = a
@@ -351,10 +346,12 @@
 
         for copy in fold1:
             copy.wait_recv()
-        edge1 = sum_slice(1)
+        terms, edge1 = sum_edges(1)
+        for j in range(2, ntiles - 2, 2):
+            sum_columns(terms, 1, j)
         for copy in fold0:
             copy.wait_recv()
-        edge0 = sum_slice(0)
+        terms, edge0 = sum_edges(0)
 
         wait_bytes(rs1.at[it, pl.ds(0, ng - 1)], p_r.at[it, 0])
         rs2_send[it] = jnp.sum(rs1[it].astype(F32), axis=0).astype(BF16)
@@ -365,12 +362,18 @@
         more = it + 1 < ITERS
         sends += fold0 + fold1 + edge0 + edge1 + halo[0] + halo[1]
         halo = [None, None]
-        for s, copies in ((1, edge1), (0, edge0)):
-            add_edges(s, copies)
-            if more:
-                steps[pl.ds(2 * s, 2)] = acc[pl.ds(2 * s, 2)].astype(BF16)
-                halo[s] = start_halo(it + 1, s, steps)
-        sq_sa[it] = squares(0) + squares(1)
+        add_edges(1, edge1)
+        if more:
+            steps[1] = acc[1].astype(BF16)
+            halo[1] = start_halo(it + 1, 1, steps.at[1])
+        for j in range(2, ntiles - 2, 2):
+            sum_columns(terms, 0, j)
+        total = squares(1, 1, inner) + squares(0, 2, inner - 2)
+        add_edges(0, edge0)
+        if more:
+            steps[0] = acc[0].astype(BF16)
+            halo[0] = start_halo(it + 1, 0, steps.at[0])
+        sq_sa[it] = total + squares(0, 1, 1) + squares(0, inner, 1)
         for j in range(1, ng):
             remote(sq_sa.at[it], sq_a.at[it, me_g], q_s.at[it, 0], q_r.at[it, 0], g_peer(j)).start()
         sq_a[it, me_g] = sq_sa[it]
@@ -381,15 +384,14 @@
             remote(ag_send.at[it], ag.at[it, me_g], p_s.at[it, 2], p_r.at[it, 2], g_peer(j)).start()
         ag[it, me_g] = ag_send[it]
 
-        if more:
-            for s in range(2):
-                own_columns(it + 1, s, steps)
-
         wait_bytes(sq_a.at[it, pl.ds(0, ng - 1)], q_r.at[it, 0])
         sq_sb[it] = jnp.sum(sq_a[it], axis=0)
         for j in range(1, nw):
             remote(sq_sb.at[it], sq_b.at[it, wi], q_s.at[it, 1], q_r.at[it, 1], w_peer(j)).start()
         sq_b[it, wi] = sq_sb[it]
+        if more:
+            for s in range(2):
+                own_columns(it + 1, s, steps.at[s])
 
         wait_bytes(ag.at[it, pl.ds(0, ng - 1)], p_r.at[it, 2])
         grad = ag[it].astype(F32).reshape(2, W, W)
@@ -400,13 +402,11 @@
         mean = jnp.sum(jnp.sum(sq_b[it], axis=0)) / cells
         scale = ETA_OBJECT * lax.rsqrt(mean + 1e-06)
 
-    stores = [pltpu.make_async_copy(probe, probe_out, local_sem.at[4])]
-    stores[0].start()
-    for c in range(4):
-        fld[c] = fld[c] - scale * acc[c, :, pl.ds(M, block_cols)]
-        store = pltpu.make_async_copy(fld.at[c], obj_out.at[c], local_sem.at[c])
-        store.start()
-        stores.append(store)
+    for s in range(2):
+        for j in range(inner):
+            here = (pl.ds(2 * s, 2), slice(None), pl.ds(j * M, M))
+            obj_out[here] = fld[here] - scale * acc[s, 1 + j].reshape(2, M, M)
+    probe_out[...] = probe[...]
     for copy in sends:
         copy.wait_send()
     for it in range(ITERS):
@@ -415,8 +415,6 @@
         wait_bytes(ag.at[it, pl.ds(0, ng - 1)], p_s.at[it, 2])
         wait_bytes(sq_a.at[it, pl.ds(0, ng - 1)], q_s.at[it, 0])
         wait_bytes(sq_b.at[it, pl.ds(0, nw - 1)], q_s.at[it, 1])
-    for store in stores:
-        store.wait()
 
 
 def per_device(object_slices, probe, patterns, offsets, owner):
@@ -426,32 +424,34 @@
     nw = 8 if npos % 8 == 0 else 2
     ng = npos // nw * ntile
     chunk = 2 * W // ng
-    grown = cols + 2 * M
+    ntiles = cols // M + 2
     cells = float(nslice * 2 * rows * cols * npos * ntile)
     dft, spread = tables()
     vmem, dma = pltpu.VMEM, pltpu.SemaphoreType.DMA
     any_space = pl.BlockSpec(memory_space=pl.ANY)
     scratch = [
-        pltpu.SMEM((bands, 2), jnp.int32),
+        pltpu.SMEM((2, bands), jnp.int32),
         pltpu.SMEM((bands,), jnp.int32),
-        pltpu.SMEM((2, bands, 2), jnp.int32),
+        pltpu.SMEM((2, 2, bands), jnp.int32),
         pltpu.SMEM((2, bands), jnp.int32),
         vmem((4, M, cols), F32),
-        vmem((4, M, grown), F32),
-        vmem((4, M, grown), BF16),
-        vmem((4, M, grown), BF16),
+        vmem((2, ntiles, 2 * M, M), F32),
+        vmem((ntiles, 2 * M, M), BF16),
+        vmem((ntiles, 2 * M, M), BF16),
+        vmem((2, ntiles, 2 * M, M), BF16),
         vmem((ITERS, 3, 2, MOST, 2, M, W), BF16),
         vmem((ITERS, 2, 2, MOST, 2, M, W), BF16),
         vmem((ITERS, 2, 2, MOST, 2, M, W), BF16),
         vmem((ITERS, 3, 2, MOST, 2, M, W), BF16),
-        vmem((ITERS, 2, 2, 2, M, W), BF16),
-        vmem((ITERS, 2, 2, 2, M, W), BF16),
+        vmem((ITERS, 2, 2, 2, 2 * M, M), BF16),
+        vmem((ITERS, 2, 2, 2, 2 * M, M), BF16),
         vmem((2, W, W), F32),
         vmem((bands, W, W), F32),
         vmem((MOST, W, W), F32),
         vmem((2, 2 * W, 2 * W), BF16),
         vmem((2, W, W), F32),
-        vmem((3 * MOST * W, grown), BF16),
+        vmem((3 * MOST, 3 * M, W), BF16),
+        vmem((3 * MOST * W, ntiles * M), BF16),
         vmem((MOST, W, 3 * M), BF16),
         vmem((MOST, 3 * M, W), BF16),
         vmem((MOST, 4, W, W), F32),
@@ -478,20 +478,8 @@
         dma((ITERS, 3)), dma((ITERS, 3)),
         dma((ITERS, 2)), dma((ITERS, 2)),
     ]
-    field, current = pl.pallas_call(
-        functools.partial(body, (npos, ntile, nw, bands, cols, cells)),
-        out_shape=(
-            jax.ShapeDtypeStruct((4, rows, cols), F32),
-            jax.ShapeDtypeStruct((2, W, W), F32),
-        ),
-        in_specs=[any_space] * 7,
-        out_specs=(any_space, any_space),
-        scratch_shapes=scratch,
-        compiler_params=pltpu.CompilerParams(
-            collective_id=0, has_side_effects=True, vmem_limit_bytes=48 * 1024 * 1024
-        ),
-    )(
-        offsets,
+    operands = (
+        offsets.T,
         owner,
         object_slices.reshape(4, rows, cols),
         probe,
@@ -499,6 +487,16 @@
         jnp.asarray(dft),
         jnp.asarray(spread),
     )
+    field, current = pl.pallas_call(
+        functools.partial(body, (npos, ntile, nw, bands, cols, cells)),
+        out_shape=(pltpu.VMEM((4, rows, cols), F32), pltpu.VMEM((2, W, W), F32)),
+        in_specs=[any_space] * 7,
+        out_specs=(pl.BlockSpec(memory_space=pltpu.VMEM),) * 2,
+        scratch_shapes=scratch,
+        compiler_params=pltpu.CompilerParams(
+            collective_id=0, has_side_effects=True, vmem_limit_bytes=48 * 1024 * 1024
+        ),
+    )(*(pltpu.with_memory_space_constraint(operand, pltpu.HBM) for operand in operands))
     return field.reshape(nslice, 2, rows, cols), current
 
 

time: 94.1 us -> 87.1 us (0.926)
  local copies, waits for them, and re-layouts: 8.07 us -> 2.11 us
    unnamed x13 -> x2, local copies, waits for them, and re-layouts: 8.07 us -> 2.11 us
where the time goes in v3:
time: 87.1 us; the launch traced here: 87 us
  Pallas kernels  84.2 us (97%)
  local copies, waits for them, and re-layouts  2.11 us (2%)
    pallas_call x1, Pallas kernels, per_device(): pl.pallas_call(functools.partial(body, (npos, ntile, nw, bands, cols, cel...  84.2 us
    unnamed x2, local copies, waits for them, and re-layouts  2.11 us

profile of v3, /device:TPU:1, one launch (start us, length us, event | category | flops | bytes accessed | tf_op | source)
XLA Modules:
  0.0 87.0 jit_solution(1138061291020206622)
XLA Ops:
  0.6 84.2 %shard_map.86 = (f32[4,128,1024]{2,1,0:T(8,128)S(1)}, f32[2,256,256]{2,1,0:T(8,128)S(1)}) custom-call(s32[2,4]{1,0:T(2,128)} %bitcast.5, s32[4]{0:T(128)} %refs_1_.1, f32[4,128,1024]{2,1,0:T(8,128)} %bitcast.4, f32[2,256,256]{2,1,0:T(8,128)} %refs_3_.1, f32[4,256,256]{2,1,0:T(8,128)} %refs_4_.1, bf16[2,512,512]{2,1,0:T(8,128)(2,1)} %constant.4.clone.refs_5_, ...), custom_call_target="tpu_custom_call" | custom-call | tf_op jit(solution)/shard_map/pallas_call | solution.py:490
  84.9 1.3 %copy.11 = f32[2,2,128,1024]{3,2,1,0:T(8,128)} copy(f32[2,2,128,1024]{3,2,1,0:T(8,128)S(1)} %bitcast.3) | data formatting | bytes 4194304
  86.2 0.8 copy.12

commit v4 on v3

--- a/solution.py
+++ b/solution.py
@@ -68,20 +68,23 @@
     (
         off, own, off_nb, own_nb, fld, acc, low0, low1, steps, parts, halo_send, fold_send, contrib, edge_send, edge_recv,
         probe, pats, wanted, tab, spread, sel, place, rows_in, rows_out, patch, x, mid, psi1, pg,
-        rs1_send, rs1, rs2_send, rs2, ag_send, ag, sq_a, sq_b, sq_sa, sq_sb,
+        pair_send, pair, rs1_send, rs1, rs2_send, rs2, ag, sq_all, sq_send,
         local_sem, info_s, info_r, col_s, col_r, halo_s, halo_r, fold_s, fold_r, edge_s, edge_r,
-        p_s, p_r, q_s, q_r,
+        p_s, p_r, q_s, q_r, pair_s, pair_r,
     ) = refs[9:]
     inner = block_cols // M
     low = (low0, low1)
     ntiles = inner + 2
     nx = npos // nw
     ng = nx * ntile
-    chunk = 2 * W // ng
+    nz = nw // 2
     p = lax.axis_index("pos")
     t = lax.axis_index("tile")
     xi, wi = p // nw, p % nw
+    zi, ci = wi // 2, wi % 2
     me_g = xi * ntile + t
+    chips = npos // 2 * ntile
+    me = p // 2 * ntile + t
 
     up = {"pos": lax.rem(p + npos - 1, npos)}
     down = {"pos": lax.rem(p + 1, npos)}
@@ -100,6 +103,14 @@
     def w_peer(j):
         return {"pos": xi * nw + lax.rem(wi + j, nw)}
 
+    def z_peer(j):
+        return {"pos": xi * nw + lax.rem(zi + j, nz) * 2 + ci}
+
+    twin = {"pos": xi * nw + zi * 2 + 1 - ci}
+
+    def chip_peer(j):
+        return {"pos": lax.rem(p + j // ntile * 2, npos), "tile": lax.rem(t + j % ntile, ntile)}
+
     def remote(src, dst, send, recv, where):
         return pltpu.make_async_remote_copy(
             src_ref=src, dst_ref=dst, send_sem=send, recv_sem=recv, device_id=where, device_id_type=MESH
@@ -111,7 +122,8 @@
     loads = [
         pltpu.make_async_copy(off_in, off, local_sem.at[0]),
         pltpu.make_async_copy(own_in, own, local_sem.at[1]),
-        pltpu.make_async_copy(obj, fld, local_sem.at[2]),
+        pltpu.make_async_copy(obj.at[pl.ds(0, 2)], fld.at[pl.ds(0, 2)], local_sem.at[2]),
+        pltpu.make_async_copy(obj.at[pl.ds(2, 2)], fld.at[pl.ds(2, 2)], local_sem.at[7]),
         pltpu.make_async_copy(pats_in, pats, local_sem.at[3]),
         pltpu.make_async_copy(probe_in, probe, local_sem.at[4]),
         pltpu.make_async_copy(tab_in, tab, local_sem.at[5]),
@@ -126,11 +138,13 @@
     friends += [w_peer(j) for j in range(1, nw)]
     for friend in friends:
         pl.semaphore_signal(barrier, inc=1, device_id=friend, device_id_type=MESH)
+    def lower(s, j):
+        low[s][1 + j] = fld[pl.ds(2 * s, 2), :, pl.ds(j * M, M)].reshape(2 * M, M).astype(BF16)
+
     for load in loads[:3]:
         load.wait()
-    for s in range(2):
-        for j in range(inner):
-            low[s][1 + j] = fld[pl.ds(2 * s, 2), :, pl.ds(j * M, M)].reshape(2 * M, M).astype(BF16)
+    for j in (0, inner - 1):
+        lower(0, j)
     pl.semaphore_wait(barrier, len(friends))
 
     info = [
@@ -143,12 +157,19 @@
         copy.start()
     cols = []
     for s in range(2):
+        if s == 1:
+            loads[3].wait()
+            for j in (0, inner - 1):
+                lower(1, j)
         cols.append([
             remote(low[s].at[inner], low[s].at[0], col_s.at[s, 0], col_r.at[s, 0], right),
             remote(low[s].at[1], low[s].at[inner + 1], col_s.at[s, 1], col_r.at[s, 1], left),
         ])
         for copy in cols[s]:
             copy.start()
+    for s in range(2):
+        for j in range(1, inner - 1):
+            lower(s, j)
     sends = info + cols[0] + cols[1]
 
     firsts = [None] * (3 * MOST)
@@ -173,18 +194,19 @@
         build_sel(k, above[k])
         build_sel(2 * MOST + k, below[k])
 
-    def chosen(source, k):
-        first = firsts[k]
+    def chosen(source, first, k):
         near = jnp.concatenate([source[first], source[first + 1], source[first + 2]], axis=1)
         return dot(near, sel[k]).astype(BF16).reshape(2, M, W)
 
     def start_halo(h, s, source):
         copies = []
-        for way, (group, part, where) in enumerate(((0, 2, up), (2, 0, down))):
+        for way in (ci, 1 - ci):
             for k in range(MOST):
-                halo_send[h, way, s, k] = chosen(source, group * MOST + k)
+                first = jnp.where(way == 0, firsts[k], firsts[2 * MOST + k])
+                halo_send[h, way, s, k] = chosen(source, first, way * (2 * MOST) + k)
             copy = remote(
-                halo_send.at[h, way, s], parts.at[h, part, s], halo_s.at[h, s, way], halo_r.at[h, s, way], where
+                halo_send.at[h, way, s], parts.at[h, 2 - 2 * way, s], halo_s.at[h, s, way], halo_r.at[h, s, way],
+                {"pos": lax.rem(p + npos - 1 + 2 * way, npos)},
             )
             copy.start()
             copies.append(copy)
@@ -192,7 +214,7 @@
 
     def own_columns(h, s, source):
         for k in range(MOST):
-            parts[h, 1, s, k] = chosen(source, MOST + k)
+            parts[h, 1, s, k] = chosen(source, firsts[MOST + k], MOST + k)
 
     def window(h, s, k, c):
         stack = jnp.concatenate([parts[h, 0, s, k, c], parts[h, 1, s, k, c], parts[h, 2, s, k, c]], axis=0)
@@ -205,7 +227,7 @@
         halo.append(start_halo(0, s, low[s]))
     for s in range(2):
         own_columns(0, s, low[s])
-    for load in loads[3:]:
+    for load in loads[4:]:
         load.wait()
     for k in range(MOST):
         found = pats[0]
@@ -230,6 +252,7 @@
         x[k, :, pl.ds(W, W)] = im.astype(BF16)
 
     for it in range(ITERS):
+        more = it + 1 < ITERS
 
         def fold_out(k, s, c, value):
             rows = dot(rows_out[k], value.astype(BF16)).astype(BF16)
@@ -238,16 +261,15 @@
             fold_send[it, 1, s, k, c] = rows[2 * M :]
 
         def start_fold(s):
-            copies = [
-                remote(
-                    fold_send.at[it, 0, s], contrib.at[it, 2, s], fold_s.at[it, s, 0], fold_r.at[it, s, 0], up
-                ),
-                remote(
-                    fold_send.at[it, 1, s], contrib.at[it, 0, s], fold_s.at[it, s, 1], fold_r.at[it, s, 1], down
-                ),
-            ]
-            for copy in copies:
+            copies = []
+            for way in (ci, 1 - ci):
+                copy = remote(
+                    fold_send.at[it, way, s], contrib.at[it, 2 - 2 * way, s],
+                    fold_s.at[it, s, way], fold_r.at[it, s, way],
+                    {"pos": lax.rem(p + npos - 1 + 2 * way, npos)},
+                )
                 copy.start()
+                copies.append(copy)
             return copies
 
         def sum_columns(terms, s, j):
@@ -262,9 +284,10 @@
             copies = []
             for way, (j, where) in enumerate(((0, left), (ntiles - 2, right))):
                 sum_columns(terms, s, j)
-                edge_send[it, way, s] = acc[s, pl.ds(j, 2)].astype(BF16)
+                tiles = pl.ds(0, 2) if more else pl.ds(way, 1)
+                edge_send[it, way, s, tiles] = acc[s, pl.ds(j, 2) if more else pl.ds(j + way, 1)].astype(BF16)
                 copy = remote(
-                    edge_send.at[it, way, s], edge_recv.at[it, 1 - way, s],
+                    edge_send.at[it, way, s, tiles], edge_recv.at[it, 1 - way, s, tiles],
                     edge_s.at[it, s, way], edge_r.at[it, s, way], where,
                 )
                 copy.start()
@@ -274,8 +297,10 @@
         def add_edges(s, copies):
             for copy in copies:
                 copy.wait_recv()
-            acc[s, pl.ds(0, 2)] = acc[s, pl.ds(0, 2)] + edge_recv[it, 0, s].astype(F32)
-            acc[s, pl.ds(ntiles - 2, 2)] = acc[s, pl.ds(ntiles - 2, 2)] + edge_recv[it, 1, s].astype(F32)
+            for way, j in ((0, 0), (1, ntiles - 2)):
+                tiles = pl.ds(0, 2) if more else pl.ds(1 - way, 1)
+                place_at = pl.ds(j, 2) if more else pl.ds(j + 1 - way, 1)
+                acc[s, place_at] = acc[s, place_at] + edge_recv[it, way, s, tiles].astype(F32)
 
         def squares(s, j, count):
             values = acc[s, pl.ds(j, count)].reshape(count * 2 * M // 8, 8, M)
@@ -299,69 +324,78 @@
             for c in range(2):
                 found = window(it, 1, k, c)
                 patch[k, 2 + c] = found if it == 0 else patch[k, 2 + c] - scale * found
+        for k in range(MOST):
+            a, b = transform(k, 1)
+            psi1[k, 0] = a
+            psi1[k, 1] = b
+            put(k, a * patch[k, 2] - b * patch[k, 3], a * patch[k, 3] + b * patch[k, 2])
+        for k in range(MOST):
+            a, b = transform(k, 0)
+            misfit = jnp.where(mine[k][3] > 0, a * a + b * b - wanted[k], 0.0)
+            put(k, misfit * a, misfit * b)
+
+        for k in range(MOST):
+            a, b = transform(k, 1)
+            put(k, patch[k, 2] * a + patch[k, 3] * b, patch[k, 2] * b - patch[k, 3] * a)
+            fold_out(k, 1, 0, psi1[k, 0] * a + psi1[k, 1] * b)
+            fold_out(k, 1, 1, psi1[k, 0] * b - psi1[k, 1] * a)
+        fold1 = start_fold(1)
+        for k in range(MOST):
+            a, b = transform(k, 0)
+            put(k, spread[0] * a + spread[1] * b, spread[0] * b - spread[1] * a)
+        for k in range(MOST):
+            a, b = transform(k, 1)
+            re = patch[k, 0] * a + patch[k, 1] * b
+            im = patch[k, 0] * b - patch[k, 1] * a
+            pg[0] = re if k == 0 else pg[0] + re
+            pg[1] = im if k == 0 else pg[1] + im
+            if k == MOST - 1:
+                pair_send[it] = pg[...].astype(BF16)
+                halves = remote(pair_send.at[it, 1 - ci], pair.at[it], pair_s.at[it, 0], pair_r.at[it, 0], twin)
+                halves.start()
+            fold_out(k, 0, 0, probe[0] * a + probe[1] * b)
+            fold_out(k, 0, 1, probe[0] * b - probe[1] * a)
+
+        halves.wait_recv()
+        rs1_send[it] = (pg[ci] + pair[it].astype(F32)).astype(BF16).reshape(ng, W // ng, W)
+        for j in range(1, ng):
+            remote(
+                rs1_send.at[it, g_index(j)], rs1.at[it, me_g], p_s.at[it, 0], p_r.at[it, 0], g_peer(j)
+            ).start()
+        fold0 = start_fold(0)
+        rs1[it, me_g] = rs1_send[it, me_g]
+
         if it > 0:
             for s in range(2):
                 for j in range(inner):
                     here = (pl.ds(2 * s, 2), slice(None), pl.ds(j * M, M))
                     fld[here] = fld[here] - scale * acc[s, 1 + j].reshape(2, M, M)
-        for k in range(MOST):
-            a, b = transform(k, 1)
-            psi1[k, 0] = a
-            psi1[k, 1] = b
-            put(k, a * patch[k, 2] - b * patch[k, 3], a * patch[k, 3] + b * patch[k, 2])
-        for k in range(MOST):
-            a, b = transform(k, 0)
-            misfit = jnp.where(mine[k][3] > 0, a * a + b * b - wanted[k], 0.0)
-            put(k, misfit * a, misfit * b)
-
-        for k in range(MOST):
-            a, b = transform(k, 1)
-            put(k, patch[k, 2] * a + patch[k, 3] * b, patch[k, 2] * b - patch[k, 3] * a)
-            fold_out(k, 1, 0, psi1[k, 0] * a + psi1[k, 1] * b)
-            fold_out(k, 1, 1, psi1[k, 0] * b - psi1[k, 1] * a)
-        fold1 = start_fold(1)
-        for k in range(MOST):
-            a, b = transform(k, 0)
-            put(k, spread[0] * a + spread[1] * b, spread[0] * b - spread[1] * a)
-        for k in range(MOST):
-            a, b = transform(k, 1)
-            fold_out(k, 0, 0, probe[0] * a + probe[1] * b)
-            fold_out(k, 0, 1, probe[0] * b - probe[1] * a)
-            re = patch[k, 0] * a + patch[k, 1] * b
-            im = patch[k, 0] * b - patch[k, 1] * a
-            if k == 0:
-                pg[pl.ds(0, W)] = re
-                pg[pl.ds(W, W)] = im
-            else:
-                pg[pl.ds(0, W)] = pg[pl.ds(0, W)] + re
-                pg[pl.ds(W, W)] = pg[pl.ds(W, W)] + im
-        fold0 = start_fold(0)
-
-        rs1_send[it] = pg[...].astype(BF16).reshape(ng, chunk, W)
-        for j in range(1, ng):
-            remote(
-                rs1_send.at[it, g_index(j)], rs1.at[it, me_g], p_s.at[it, 0], p_r.at[it, 0], g_peer(j)
-            ).start()
-        rs1[it, me_g] = rs1_send[it, me_g]
-
         for copy in fold1:
             copy.wait_recv()
         terms, edge1 = sum_edges(1)
         for j in range(2, ntiles - 2, 2):
             sum_columns(terms, 1, j)
+
+        wait_bytes(rs1.at[it, pl.ds(0, ng - 1)], p_r.at[it, 0])
+        rs2_send[it] = jnp.sum(rs1[it].astype(F32), axis=0).astype(BF16)
+        for j in range(1, nz):
+            remote(rs2_send.at[it], rs2.at[it, zi], p_s.at[it, 1], p_r.at[it, 1], z_peer(j)).start()
+        rs2[it, zi] = rs2_send[it]
+
         for copy in fold0:
             copy.wait_recv()
         terms, edge0 = sum_edges(0)
 
-        wait_bytes(rs1.at[it, pl.ds(0, ng - 1)], p_r.at[it, 0])
-        rs2_send[it] = jnp.sum(rs1[it].astype(F32), axis=0).astype(BF16)
-        for j in range(1, nw):
-            remote(rs2_send.at[it], rs2.at[it, wi], p_s.at[it, 1], p_r.at[it, 1], w_peer(j)).start()
-        rs2[it, wi] = rs2_send[it]
-
-        more = it + 1 < ITERS
         sends += fold0 + fold1 + edge0 + edge1 + halo[0] + halo[1]
         halo = [None, None]
+        if nz > 1:
+            wait_bytes(rs2.at[it, pl.ds(0, nz - 1)], p_r.at[it, 1])
+        ag[it, ci, me_g] = jnp.sum(rs2[it].astype(F32), axis=0).astype(BF16)
+        for j in range(1, ng):
+            remote(
+                ag.at[it, ci, me_g], ag.at[it, ci, me_g], p_s.at[it, 2], p_r.at[it, 2], g_peer(j)
+            ).start()
+
         add_edges(1, edge1)
         if more:
             steps[1] = acc[1].astype(BF16)
@@ -370,36 +404,34 @@
             sum_columns(terms, 0, j)
         total = squares(1, 1, inner) + squares(0, 2, inner - 2)
         add_edges(0, edge0)
+        sq_send[it, 0] = jnp.sum(total + squares(0, 1, 1) + squares(0, inner, 1), axis=0, keepdims=True)
+        both = remote(sq_send.at[it, 0], sq_send.at[it, 1], pair_s.at[it, 2], pair_r.at[it, 2], twin)
+        both.start()
         if more:
             steps[0] = acc[0].astype(BF16)
+        both.wait_recv()
+        sends += [both]
+        sq_send[it, 2] = sq_send[it, 0] + sq_send[it, 1]
+        for j in range(1, chips):
+            remote(sq_send.at[it, 2], sq_all.at[it, me], q_s.at[it], q_r.at[it], chip_peer(j)).start()
+        sq_all[it, me] = sq_send[it, 2]
+        if more:
             halo[0] = start_halo(it + 1, 0, steps.at[0])
-        sq_sa[it] = total + squares(0, 1, 1) + squares(0, inner, 1)
-        for j in range(1, ng):
-            remote(sq_sa.at[it], sq_a.at[it, me_g], q_s.at[it, 0], q_r.at[it, 0], g_peer(j)).start()
-        sq_a[it, me_g] = sq_sa[it]
-
-        wait_bytes(rs2.at[it, pl.ds(0, nw - 1)], p_r.at[it, 1])
-        ag_send[it] = jnp.sum(rs2[it].astype(F32), axis=0).astype(BF16)
-        for j in range(1, ng):
-            remote(ag_send.at[it], ag.at[it, me_g], p_s.at[it, 2], p_r.at[it, 2], g_peer(j)).start()
-        ag[it, me_g] = ag_send[it]
-
-        wait_bytes(sq_a.at[it, pl.ds(0, ng - 1)], q_r.at[it, 0])
-        sq_sb[it] = jnp.sum(sq_a[it], axis=0)
-        for j in range(1, nw):
-            remote(sq_sb.at[it], sq_b.at[it, wi], q_s.at[it, 1], q_r.at[it, 1], w_peer(j)).start()
-        sq_b[it, wi] = sq_sb[it]
+
+        wait_bytes(rs1.at[it, pl.ds(0, ng - 1)], p_r.at[it, 2])
+        whole = remote(ag.at[it, ci], ag.at[it, ci], pair_s.at[it, 1], pair_r.at[it, 1], twin)
+        whole.start()
         if more:
             for s in range(2):
                 own_columns(it + 1, s, steps.at[s])
-
-        wait_bytes(ag.at[it, pl.ds(0, ng - 1)], p_r.at[it, 2])
+        whole.wait_recv()
+        sends += [halves, whole]
         grad = ag[it].astype(F32).reshape(2, W, W)
         mean = jnp.sum(grad * grad) / float(2 * W * W)
         probe[...] = probe[...] - ETA_PROBE * lax.rsqrt(mean + 1e-06) * grad
 
-        wait_bytes(sq_b.at[it, pl.ds(0, nw - 1)], q_r.at[it, 1])
-        mean = jnp.sum(jnp.sum(sq_b[it], axis=0)) / cells
+        wait_bytes(sq_all.at[it, pl.ds(0, chips - 1)], q_r.at[it])
+        mean = jnp.sum(jnp.sum(sq_all[it], axis=0)) / cells
         scale = ETA_OBJECT * lax.rsqrt(mean + 1e-06)
 
     for s in range(2):
@@ -410,11 +442,11 @@
     for copy in sends:
         copy.wait_send()
     for it in range(ITERS):
-        wait_bytes(rs1_send.at[it, pl.ds(0, ng - 1)], p_s.at[it, 0])
-        wait_bytes(rs2.at[it, pl.ds(0, nw - 1)], p_s.at[it, 1])
-        wait_bytes(ag.at[it, pl.ds(0, ng - 1)], p_s.at[it, 2])
-        wait_bytes(sq_a.at[it, pl.ds(0, ng - 1)], q_s.at[it, 0])
-        wait_bytes(sq_b.at[it, pl.ds(0, nw - 1)], q_s.at[it, 1])
+        wait_bytes(rs1.at[it, pl.ds(0, ng - 1)], p_s.at[it, 0])
+        if nz > 1:
+            wait_bytes(rs2.at[it, pl.ds(0, nz - 1)], p_s.at[it, 1])
+        wait_bytes(rs1.at[it, pl.ds(0, ng - 1)], p_s.at[it, 2])
+        wait_bytes(sq_all.at[it, pl.ds(0, chips - 1)], q_s.at[it])
 
 
 def per_device(object_slices, probe, patterns, offsets, owner):
@@ -423,7 +455,6 @@
     npos, ntile = lax.axis_size("pos"), lax.axis_size("tile")
     nw = 8 if npos % 8 == 0 else 2
     ng = npos // nw * ntile
-    chunk = 2 * W // ng
     ntiles = cols // M + 2
     cells = float(nslice * 2 * rows * cols * npos * ntile)
     dft, spread = tables()
@@ -458,25 +489,25 @@
         vmem((MOST, W, 2 * W), BF16),
         vmem((MOST, 2 * W, W), BF16),
         vmem((MOST, 2, W, W), F32),
-        vmem((2 * W, W), F32),
-        vmem((ITERS, ng, chunk, W), BF16),
-        vmem((ITERS, ng, chunk, W), BF16),
-        vmem((ITERS, chunk, W), BF16),
-        vmem((ITERS, nw, chunk, W), BF16),
-        vmem((ITERS, chunk, W), BF16),
-        vmem((ITERS, ng, chunk, W), BF16),
-        vmem((ITERS, ng, 8, M), F32),
-        vmem((ITERS, nw, 8, M), F32),
-        vmem((ITERS, 8, M), F32),
-        vmem((ITERS, 8, M), F32),
-        dma((7,)),
+        vmem((2, W, W), F32),
+        vmem((ITERS, 2, W, W), BF16),
+        vmem((ITERS, W, W), BF16),
+        vmem((ITERS, ng, W // ng, W), BF16),
+        vmem((ITERS, ng, W // ng, W), BF16),
+        vmem((ITERS, W // ng, W), BF16),
+        vmem((ITERS, nw // 2, W // ng, W), BF16),
+        vmem((ITERS, 2, ng, W // ng, W), BF16),
+        vmem((ITERS, npos // 2 * ntile, 1, M), F32),
+        vmem((ITERS, 3, 1, M), F32),
+        dma((8,)),
         dma((4,)), dma((4,)),
         dma((2, 2)), dma((2, 2)),
         dma((ITERS, 2, 2)), dma((ITERS, 2, 2)),
         dma((ITERS, 2, 2)), dma((ITERS, 2, 2)),
         dma((ITERS, 2, 2)), dma((ITERS, 2, 2)),
         dma((ITERS, 3)), dma((ITERS, 3)),
-        dma((ITERS, 2)), dma((ITERS, 2)),
+        dma((ITERS,)), dma((ITERS,)),
+        dma((ITERS, 3)), dma((ITERS, 3)),
     ]
     operands = (
         offsets.T,

time: 87.1 us -> 80.8 us (0.928)
  Pallas kernels: 84.2 us -> 77.4 us
    pallas_call x1, Pallas kernels: 84.2 us -> 77.4 us  [per_device(): pl.pallas_call(functools.partial(body, (npos, ntile, nw, bands, cols, cel...]
where the time goes in v4:
time: 80.8 us; the launch traced here: 80.2 us
  Pallas kernels  77.4 us (96%)
  local copies, waits for them, and re-layouts  2.11 us (3%)
    pallas_call x1, Pallas kernels, per_device(): pl.pallas_call(functools.partial(body, (npos, ntile, nw, bands, cols, cel...  77.4 us
    unnamed x2, local copies, waits for them, and re-layouts  2.11 us

profile of v4, /device:TPU:1, one launch (start us, length us, event | category | flops | bytes accessed | tf_op | source)
XLA Modules:
  0.0 80.2 jit_solution(18036836858859453256)
XLA Ops:
  0.6 77.4 %shard_map.86 = (f32[4,128,1024]{2,1,0:T(8,128)S(1)}, f32[2,256,256]{2,1,0:T(8,128)S(1)}) custom-call(s32[2,4]{1,0:T(2,128)} %bitcast.5, s32[4]{0:T(128)} %refs_1_.1, f32[4,128,1024]{2,1,0:T(8,128)} %bitcast.4, f32[2,256,256]{2,1,0:T(8,128)} %refs_3_.1, f32[4,256,256]{2,1,0:T(8,128)} %refs_4_.1, bf16[2,512,512]{2,1,0:T(8,128)(2,1)} %constant.4.clone.refs_5_, ...), custom_call_target="tpu_custom_call" | custom-call | tf_op jit(solution)/shard_map/pallas_call | solution.py:521
  78.1 1.3 %copy.11 = f32[2,2,128,1024]{3,2,1,0:T(8,128)} copy(f32[2,2,128,1024]{3,2,1,0:T(8,128)S(1)} %bitcast.3) | data formatting | bytes 4194304
  79.4 0.8 copy.12

commit v5 on v4

--- a/solution.py
+++ b/solution.py
@@ -198,12 +198,15 @@
         near = jnp.concatenate([source[first], source[first + 1], source[first + 2]], axis=1)
         return dot(near, sel[k]).astype(BF16).reshape(2, M, W)
 
-    def start_halo(h, s, source):
+    def start_halo(h, s, source, first_of_all=None):
         copies = []
         for way in (ci, 1 - ci):
             for k in range(MOST):
                 first = jnp.where(way == 0, firsts[k], firsts[2 * MOST + k])
                 halo_send[h, way, s, k] = chosen(source, first, way * (2 * MOST) + k)
+            if first_of_all is not None:
+                first_of_all()
+                first_of_all = None
             copy = remote(
                 halo_send.at[h, way, s], parts.at[h, 2 - 2 * way, s], halo_s.at[h, s, way], halo_r.at[h, s, way],
                 {"pos": lax.rem(p + npos - 1 + 2 * way, npos)},
@@ -260,12 +263,12 @@
             contrib[it, 1, s, k, c] = rows[M : 2 * M]
             fold_send[it, 1, s, k, c] = rows[2 * M :]
 
-        def start_fold(s):
+        def start_fold(s, k):
             copies = []
             for way in (ci, 1 - ci):
                 copy = remote(
-                    fold_send.at[it, way, s], contrib.at[it, 2 - 2 * way, s],
-                    fold_s.at[it, s, way], fold_r.at[it, s, way],
+                    fold_send.at[it, way, s, k], contrib.at[it, 2 - 2 * way, s, k],
+                    fold_s.at[it, s, k, way], fold_r.at[it, s, k, way],
                     {"pos": lax.rem(p + npos - 1 + 2 * way, npos)},
                 )
                 copy.start()
@@ -339,7 +342,7 @@
             put(k, patch[k, 2] * a + patch[k, 3] * b, patch[k, 2] * b - patch[k, 3] * a)
             fold_out(k, 1, 0, psi1[k, 0] * a + psi1[k, 1] * b)
             fold_out(k, 1, 1, psi1[k, 0] * b - psi1[k, 1] * a)
-        fold1 = start_fold(1)
+            fold1 = start_fold(1, k) + (fold1 if k > 0 else [])
         for k in range(MOST):
             a, b = transform(k, 0)
             put(k, spread[0] * a + spread[1] * b, spread[0] * b - spread[1] * a)
@@ -355,6 +358,8 @@
                 halves.start()
             fold_out(k, 0, 0, probe[0] * a + probe[1] * b)
             fold_out(k, 0, 1, probe[0] * b - probe[1] * a)
+            if k == 0:
+                fold0 = start_fold(0, 0)
 
         halves.wait_recv()
         rs1_send[it] = (pg[ci] + pair[it].astype(F32)).astype(BF16).reshape(ng, W // ng, W)
@@ -362,7 +367,7 @@
             remote(
                 rs1_send.at[it, g_index(j)], rs1.at[it, me_g], p_s.at[it, 0], p_r.at[it, 0], g_peer(j)
             ).start()
-        fold0 = start_fold(0)
+        fold0 += start_fold(0, 1)
         rs1[it, me_g] = rs1_send[it, me_g]
 
         if it > 0:
@@ -407,16 +412,20 @@
         sq_send[it, 0] = jnp.sum(total + squares(0, 1, 1) + squares(0, inner, 1), axis=0, keepdims=True)
         both = remote(sq_send.at[it, 0], sq_send.at[it, 1], pair_s.at[it, 2], pair_r.at[it, 2], twin)
         both.start()
+        sends += [both]
+
+        def send_squares():
+            both.wait_recv()
+            sq_send[it, 2] = sq_send[it, 0] + sq_send[it, 1]
+            for j in range(1, chips):
+                remote(sq_send.at[it, 2], sq_all.at[it, me], q_s.at[it], q_r.at[it], chip_peer(j)).start()
+            sq_all[it, me] = sq_send[it, 2]
+
         if more:
             steps[0] = acc[0].astype(BF16)
-        both.wait_recv()
-        sends += [both]
-        sq_send[it, 2] = sq_send[it, 0] + sq_send[it, 1]
-        for j in range(1, chips):
-            remote(sq_send.at[it, 2], sq_all.at[it, me], q_s.at[it], q_r.at[it], chip_peer(j)).start()
-        sq_all[it, me] = sq_send[it, 2]
-        if more:
-            halo[0] = start_halo(it + 1, 0, steps.at[0])
+            halo[0] = start_halo(it + 1, 0, steps.at[0], send_squares)
+        else:
+            send_squares()
 
         wait_bytes(rs1.at[it, pl.ds(0, ng - 1)], p_r.at[it, 2])
         whole = remote(ag.at[it, ci], ag.at[it, ci], pair_s.at[it, 1], pair_r.at[it, 1], twin)
@@ -503,7 +512,7 @@
         dma((4,)), dma((4,)),
         dma((2, 2)), dma((2, 2)),
         dma((ITERS, 2, 2)), dma((ITERS, 2, 2)),
-        dma((ITERS, 2, 2)), dma((ITERS, 2, 2)),
+        dma((ITERS, 2, MOST, 2)), dma((ITERS, 2, MOST, 2)),
         dma((ITERS, 2, 2)), dma((ITERS, 2, 2)),
         dma((ITERS, 3)), dma((ITERS, 3)),
         dma((ITERS,)), dma((ITERS,)),

time: 80.8 us -> 77.9 us (0.964)
  Pallas kernels: 77.4 us -> 74.8 us
    pallas_call x1, Pallas kernels: 77.4 us -> 74.8 us  [per_device(): pl.pallas_call(functools.partial(body, (npos, ntile, nw, bands, cols, cel...]
where the time goes in v5:
time: 77.9 us; the launch traced here: 77.6 us
  Pallas kernels  74.8 us (96%)
  local copies, waits for them, and re-layouts  2.11 us (3%)
    pallas_call x1, Pallas kernels, per_device(): pl.pallas_call(functools.partial(body, (npos, ntile, nw, bands, cols, cel...  74.8 us
    unnamed x2, local copies, waits for them, and re-layouts  2.11 us

profile of v5, /device:TPU:1, one launch (start us, length us, event | category | flops | bytes accessed | tf_op | source)
XLA Modules:
  0.0 77.6 jit_solution(10187399814866068890)
XLA Ops:
  0.6 74.8 %shard_map.86 = (f32[4,128,1024]{2,1,0:T(8,128)S(1)}, f32[2,256,256]{2,1,0:T(8,128)S(1)}) custom-call(s32[2,4]{1,0:T(2,128)} %bitcast.5, s32[4]{0:T(128)} %refs_1_.1, f32[4,128,1024]{2,1,0:T(8,128)} %bitcast.4, f32[2,256,256]{2,1,0:T(8,128)} %refs_3_.1, f32[4,256,256]{2,1,0:T(8,128)} %refs_4_.1, bf16[2,512,512]{2,1,0:T(8,128)(2,1)} %constant.4.clone.refs_5_, ...), custom_call_target="tpu_custom_call" | custom-call | tf_op jit(solution)/shard_map/pallas_call | solution.py:530
  75.5 1.3 %copy.11 = f32[2,2,128,1024]{3,2,1,0:T(8,128)} copy(f32[2,2,128,1024]{3,2,1,0:T(8,128)S(1)} %bitcast.3) | data formatting | bytes 4194304
  76.8 0.8 %copy.12 = f32[2,256,256]{2,1,0:T(8,128)} copy(f32[2,256,256]{2,1,0:T(8,128)S(1)} %get-tuple-element.7) | data formatting | bytes 1048576

commit v6 on v5

--- a/solution.py
+++ b/solution.py
@@ -390,6 +390,8 @@
         for copy in fold0:
             copy.wait_recv()
         terms, edge0 = sum_edges(0)
+        for j in range(2, ntiles - 2, 2):
+            sum_columns(terms, 0, j)
 
         sends += fold0 + fold1 + edge0 + edge1 + halo[0] + halo[1]
         halo = [None, None]
@@ -405,8 +407,6 @@
         if more:
             steps[1] = acc[1].astype(BF16)
             halo[1] = start_halo(it + 1, 1, steps.at[1])
-        for j in range(2, ntiles - 2, 2):
-            sum_columns(terms, 0, j)
         total = squares(1, 1, inner) + squares(0, 2, inner - 2)
         add_edges(0, edge0)
         sq_send[it, 0] = jnp.sum(total + squares(0, 1, 1) + squares(0, inner, 1), axis=0, keepdims=True)

time: 77.9 us -> 78.4 us (level)
  no operation moved by 1% of the time
where the time goes in v6:
time: 78.4 us; the launch traced here: 77.7 us
  Pallas kernels  75 us (96%)
  local copies, waits for them, and re-layouts  2.11 us (3%)
    pallas_call x1, Pallas kernels, per_device(): pl.pallas_call(functools.partial(body, (npos, ntile, nw, bands, cols, cel...  75 us
    unnamed x2, local copies, waits for them, and re-layouts  2.11 us

profile of v6, /device:TPU:1, one launch (start us, length us, event | category | flops | bytes accessed | tf_op | source)
XLA Modules:
  0.0 77.7 jit_solution(8807432672946214111)
XLA Ops:
  0.6 75.0 %shard_map.86 = (f32[4,128,1024]{2,1,0:T(8,128)S(1)}, f32[2,256,256]{2,1,0:T(8,128)S(1)}) custom-call(s32[2,4]{1,0:T(2,128)} %bitcast.5, s32[4]{0:T(128)} %refs_1_.1, f32[4,128,1024]{2,1,0:T(8,128)} %bitcast.4, f32[2,256,256]{2,1,0:T(8,128)} %refs_3_.1, f32[4,256,256]{2,1,0:T(8,128)} %refs_4_.1, bf16[2,512,512]{2,1,0:T(8,128)(2,1)} %constant.4.clone.refs_5_, ...), custom_call_target="tpu_custom_call" | custom-call | tf_op jit(solution)/shard_map/pallas_call | solution.py:530
  75.6 1.3 %copy.11 = f32[2,2,128,1024]{3,2,1,0:T(8,128)} copy(f32[2,2,128,1024]{3,2,1,0:T(8,128)S(1)} %bitcast.3) | data formatting | bytes 4194304
  76.9 0.8 %copy.12 = f32[2,256,256]{2,1,0:T(8,128)} copy(f32[2,256,256]{2,1,0:T(8,128)S(1)} %get-tuple-element.7) | data formatting | bytes 1048576
